TPU v7x, 32 devices: a whole 2x2x4 slice. The times are simulated.
32 devices in a mesh: dp: 8 (over z, x), mp: 4 (over y, core).
Axes of the slice: x: 2, y: 2, z: 4, core: 2. Of those that a mesh axis runs over, the one named last changes fastest.
Arguments:
- tokens: bfloat16 [4096, 1536], P(('dp', 'mp')), may hold values from -6 to 6
- cotangent: bfloat16 [4096, 1536], P(('dp', 'mp')), may hold values from -6 to 6
- doc_starts: int32 [8, 7], P('dp'), may hold values from 0 to 511, as said below
- valid_len: int32 [8], P('dp'), may hold values from 449 to 512
- gain_mixer: float32 [1536], replicated, may hold values from 0.5 to 1.5
- mixer_in_x: bfloat16 [1536, 3072], P(None, 'mp'), may hold values from -0.15625 to 0.15625
- mixer_in_z: bfloat16 [1536, 3072], P(None, 'mp'), may hold values from -0.15625 to 0.15625
- conv_weight: float32 [4, 3072], P(None, 'mp'), may hold values from -3 to 3
- conv_bias: float32 [3072], P('mp'), may hold values from -3 to 3
- mixer_proj: bfloat16 [3072, 128], P('mp'), may hold values from -0.109375 to 0.109375
- delta_proj: bfloat16 [96, 3072], P(None, 'mp'), may hold values from -0.625 to 0.625
- delta_bias: float32 [3072], P('mp'), may hold values from -4.6 to -1
- decay_log: float32 [3072, 16], P('mp'), may hold values from 0 to 2.77
- skip_weight: float32 [3072], P('mp'), may hold values from 0.5 to 1.5
- mixer_out: bfloat16 [3072, 1536], P('mp'), may hold values from -0.4375 to 0.4375
- gain_first: float32 [1536], replicated, may hold values from 0.5 to 1.5
- gate_first: bfloat16 [1536, 4096], P(None, 'mp'), may hold values from -0.15625 to 0.15625
- up_first: bfloat16 [1536, 4096], P(None, 'mp'), may hold values from -0.15625 to 0.15625
- down_first: bfloat16 [4096, 1536], P('mp'), may hold values from -0.09375 to 0.09375
- gain_attn: float32 [1536], replicated, may hold values from 0.5 to 1.5
- query_weight: bfloat16 [1536, 1536], P(None, 'mp'), may hold values from -0.15625 to 0.15625
- key_weight: bfloat16 [1536, 1536], P(None, 'mp'), may hold values from -0.15625 to 0.15625
- value_weight: bfloat16 [1536, 1536], P(None, 'mp'), may hold values from -0.15625 to 0.15625
- output_weight: bfloat16 [1536, 1536], P('mp'), may hold values from -0.625 to 0.625
- gain_second: float32 [1536], replicated, may hold values from 0.5 to 1.5
- gate_second: bfloat16 [1536, 4096], P(None, 'mp'), may hold values from -0.15625 to 0.15625
- up_second: bfloat16 [1536, 4096], P(None, 'mp'), may hold values from -0.15625 to 0.15625
- down_second: bfloat16 [4096, 1536], P('mp'), may hold values from -0.09375 to 0.09375
Outputs:
- mixed_out: bfloat16 [4096, 1536], P(('dp', 'mp'))
- input_grad: float32 [4096, 1536], P(('dp', 'mp'))
- grad_gain_mixer: float32 [1536], replicated
- grad_mixer_in_x: float32 [1536, 3072], P(None, 'mp')
- grad_mixer_in_z: float32 [1536, 3072], P(None, 'mp')
- grad_conv_weight: float32 [4, 3072], P(None, 'mp')
- grad_conv_bias: float32 [3072], P('mp')
- grad_mixer_proj: float32 [3072, 128], P('mp')
- grad_delta_proj: float32 [96, 3072], P(None, 'mp')
- grad_delta_bias: float32 [3072], P('mp')
- grad_decay_log: float32 [3072, 16], P('mp')
- grad_skip_weight: float32 [3072], P('mp')
- grad_mixer_out: float32 [3072, 1536], P('mp')
- grad_gain_first: float32 [1536], replicated
- grad_gate_first: float32 [1536, 4096], P(None, 'mp')
- grad_up_first: float32 [1536, 4096], P(None, 'mp')
- grad_down_first: float32 [4096, 1536], P('mp')
- grad_gain_attn: float32 [1536], replicated
- grad_query_weight: float32 [1536, 1536], P(None, 'mp')
- grad_key_weight: float32 [1536, 1536], P(None, 'mp')
- grad_value_weight: float32 [1536, 1536], P(None, 'mp')
- grad_output_weight: float32 [1536, 1536], P('mp')
- grad_gain_second: float32 [1536], replicated
- grad_gate_second: float32 [1536, 4096], P(None, 'mp')
- grad_up_second: float32 [1536, 4096], P(None, 'mp')
- grad_down_second: float32 [4096, 1536], P('mp')
Inputs may be any that keep to these rules, and one draw needn't show every extreme that they name: `doc_starts`: in each row the entries rise strictly from a first entry of 0, and all lie below the row's valid_len; some row has a document starting at 511.
All inputs are finite; a program needn't handle non-finite values.
Results may differ from a plain program's by a relative error of at most 0.033.
Values may be sent and summed in bfloat16 or wider, within the bound.
No kernel may reach another device: no remote copies, remote signals or barrier semaphores. Data moves between devices by JAX's collectives and lax.ppermute only.
A program may use at most 448 MiB of HBM per device.

v0:
```python
import math

import jax
import jax.numpy as jnp
from jax import lax
from jax.sharding import PartitionSpec as P

STATE = 16
CONV = 4
RANK = 96
HDIM = 128
WINDOW = 2048
BLOCK_ROWS = 512
SCAN_BLOCK = 16


EPSILON = 1e-05
MASKED = -1e30


def product(left_rows, weight):
    return jnp.dot(left_rows, weight, preferred_element_type=jnp.float32)


def left_product(left_rows, right_rows):
    return lax.dot_general(
        left_rows, right_rows, (((0,), (0,)), ((), ())), preferred_element_type=jnp.float32
    )


def right_product(left_rows, weight):
    return lax.dot_general(
        left_rows, weight, (((1,), (1,)), ((), ())), preferred_element_type=jnp.float32
    )


def rms_apply(stream, gain_vec):
    return (
        stream * lax.rsqrt(jnp.mean(stream * stream, axis=-1, keepdims=True) + EPSILON) * gain_vec
    )


def document_ids(starts, length, seq_len):
    places = jnp.arange(seq_len, dtype=jnp.int32)
    counted = jnp.sum((starts[None, :] <= places[:, None]).astype(jnp.int32), axis=1) - 1
    return jnp.where(places < length, counted, starts.shape[0])


def causal_conv(mixer_x, conv_weight, conv_bias, documents):
    running_sum = conv_bias[None, :] + conv_weight[0][None, :] * mixer_x
    for lag_steps in range(1, CONV):
        shifted = jnp.concatenate(
            [jnp.zeros((lag_steps, mixer_x.shape[1]), mixer_x.dtype), mixer_x[:-lag_steps]], axis=0
        )
        before = jnp.concatenate([jnp.full((lag_steps,), -1, jnp.int32), documents[:-lag_steps]])
        same_doc = (before == documents).astype(mixer_x.dtype)
        running_sum = running_sum + conv_weight[lag_steps][None, :] * shifted * same_doc[:, None]
    return jax.nn.silu(running_sum)


def selective_scan(
    activated, delta_pre, input_map, output_map, decay_log, skip_weight, gating, carry_on
):
    seq_len, channels = activated.shape
    delta_time = jax.nn.softplus(delta_pre)
    decay_rates = -jnp.exp(decay_log)
    block_count = seq_len // SCAN_BLOCK

    def one_block(hidden_state, pieces):
        act_block, delta_block, in_block, out_block, keep_block = pieces
        readouts = []
        for position in range(SCAN_BLOCK):
            factor = jnp.exp(delta_block[position][:, None] * decay_rates)
            hidden_state = (
                keep_block[position] * factor * hidden_state
                + (delta_block[position] * act_block[position])[:, None]
                * in_block[position][None, :]
            )
            readouts.append(jnp.sum(hidden_state * out_block[position][None, :], axis=1))
        return (hidden_state, jnp.stack(readouts))

    pieces = (
        activated.reshape(block_count, SCAN_BLOCK, channels),
        delta_time.reshape(block_count, SCAN_BLOCK, channels),
        input_map.reshape(block_count, SCAN_BLOCK, -1),
        output_map.reshape(block_count, SCAN_BLOCK, -1),
        carry_on.reshape(block_count, SCAN_BLOCK),
    )
    initial = jnp.zeros((channels, decay_log.shape[1]), jnp.float32)
    _, readouts = lax.scan(jax.checkpoint(one_block), initial, pieces)
    result = readouts.reshape(seq_len, channels) + skip_weight[None, :] * activated
    return result * jax.nn.silu(gating)


def visible(start_row, block_rows, documents):
    places = jnp.arange(documents.shape[0], dtype=jnp.int32)
    row_pos = start_row + jnp.arange(block_rows, dtype=jnp.int32)
    return (
        (places[None, :] <= row_pos[:, None])
        & (row_pos[:, None] - places[None, :] < WINDOW)
        & (documents[None, :] == documents[:, None])
    )


def attend_forward(queries, key_rows, value_rows, documents):
    seq_len, head_count, _ = queries.shape
    block_rows = min(BLOCK_ROWS, seq_len)
    score_scale = HDIM ** (-0.5)

    def one_block(start_row):
        allowed = visible(start_row, block_rows, documents)
        scores = (
            jnp.einsum("qhd,khd->hqk", queries, key_rows, preferred_element_type=jnp.float32)
            * score_scale
        )
        scores = jnp.where(allowed[None], scores, MASKED)
        row_max = jnp.max(scores, axis=-1, keepdims=True)
        weights = jnp.exp(scores - row_max)
        normalizer = jnp.sum(weights, axis=-1, keepdims=True)
        attn_probs = (weights / normalizer).astype(jnp.bfloat16)
        result = jnp.einsum(
            "hqk,khd->qhd", attn_probs, value_rows, preferred_element_type=jnp.float32
        )
        return (result.astype(jnp.bfloat16), row_max[..., 0] + jnp.log(normalizer[..., 0]))

    starts = jnp.arange(seq_len // block_rows) * block_rows
    result, log_norm = lax.map(one_block, starts)
    return (result.reshape(seq_len, head_count, HDIM), log_norm)


def attend_backward(queries, key_rows, value_rows, documents, log_norm, d_attended):
    seq_len = queries.shape[0]
    block_rows = min(BLOCK_ROWS, seq_len)
    score_scale = HDIM ** (-0.5)

    def one_block(carried, pieces):
        d_keys, d_values = carried
        start_row, norm_block = pieces
        allowed = visible(start_row, block_rows, documents)
        scores = (
            jnp.einsum("qhd,khd->hqk", queries, key_rows, preferred_element_type=jnp.float32)
            * score_scale
        )
        scores = jnp.where(allowed[None], scores, MASKED)
        attn_probs = jnp.exp(scores - norm_block[..., None])
        d_probs = jnp.einsum(
            "qhd,khd->hqk", d_attended, value_rows, preferred_element_type=jnp.float32
        )
        d_scores = (
            attn_probs * (d_probs - jnp.sum(attn_probs * d_probs, axis=-1, keepdims=True))
        ).astype(jnp.bfloat16)
        d_query = (
            jnp.einsum("hqk,khd->qhd", d_scores, key_rows, preferred_element_type=jnp.float32)
            * score_scale
        )
        d_keys = (
            d_keys
            + jnp.einsum("hqk,qhd->khd", d_scores, queries, preferred_element_type=jnp.float32)
            * score_scale
        )
        d_values = d_values + jnp.einsum(
            "hqk,qhd->khd",
            attn_probs.astype(jnp.bfloat16),
            d_attended,
            preferred_element_type=jnp.float32,
        )
        return ((d_keys, d_values), d_query)

    starts = jnp.arange(seq_len // block_rows) * block_rows
    zero_rows = jnp.zeros(key_rows.shape, jnp.float32)
    (d_keys, d_values), d_queries = lax.scan(one_block, (zero_rows, zero_rows), (starts, log_norm))
    return (d_queries.reshape(queries.shape), d_keys, d_values)


def reduce_rows(parts):
    piece_shapes = [piece.shape for piece in parts]
    flattened = jnp.concatenate([piece.reshape(-1) for piece in parts])
    row_unit = lax.axis_size("dp") * 128
    padding = -flattened.shape[0] % row_unit
    grid_rows = jnp.pad(flattened, (0, padding)).reshape(-1, 128)
    summed_all = lax.all_gather(
        lax.psum_scatter(grid_rows, "dp", scatter_dimension=0, tiled=True).astype(jnp.bfloat16),
        "dp",
        axis=0,
        tiled=True,
    ).astype(jnp.float32)
    summed_all = summed_all.reshape(-1)
    result = []
    offset = 0
    for piece_shape in piece_shapes:
        element_count = math.prod(piece_shape)
        result.append(summed_all[offset : offset + element_count].reshape(piece_shape))
        offset = offset + element_count
    return result


def per_device(
    tokens,
    cotangent,
    doc_starts,
    valid_len,
    gain_mixer,
    mixer_in_x,
    mixer_in_z,
    conv_weight,
    conv_bias,
    mixer_proj,
    delta_proj,
    delta_bias,
    decay_log,
    skip_weight,
    mixer_out,
    gain_first,
    gate_first,
    up_first,
    down_first,
    gain_attn,
    query_weight,
    key_weight,
    value_weight,
    output_weight,
    gain_second,
    gate_second,
    up_second,
    down_second,
):
    local_rows = tokens.shape[0]
    seq_len = local_rows * lax.axis_size("mp")
    documents = document_ids(doc_starts[0], valid_len[0], seq_len)
    before = jnp.concatenate([jnp.full((1,), -1, jnp.int32), documents[:-1]])
    carry_on = (before == documents).astype(jnp.float32)

    def spread(normed):
        return lax.all_gather(normed, "mp", axis=0, tiled=True)

    def spread_grad(stream_grad):
        return lax.all_gather(stream_grad.astype(jnp.bfloat16), "mp", axis=0, tiled=True)

    def collect(left_rows, weight):

        def term(row_start, row_count):
            return product(lax.dynamic_slice_in_dim(left_rows, row_start, row_count, 0), weight)

        return lax.psum_scatter(
            term(jnp.int32(0), local_rows * lax.axis_size("mp")).astype(jnp.bfloat16),
            "mp",
            scatter_dimension=0,
            tiled=True,
        ).astype(jnp.float32)

    def collect_back(term_pairs):

        def term(row_start, row_count):
            running_sum = jnp.zeros((row_count, term_pairs[0][1].shape[0]), jnp.float32)
            for left_rows, weight in term_pairs:
                running_sum = running_sum + right_product(
                    lax.dynamic_slice_in_dim(left_rows, row_start, row_count, 0), weight
                )
            return running_sum

        return lax.psum_scatter(
            term(jnp.int32(0), local_rows * lax.axis_size("mp")).astype(jnp.bfloat16),
            "mp",
            scatter_dimension=0,
            tiled=True,
        ).astype(jnp.float32)

    def ffn_forward(stream, gain_vec, gate_w, up_w, down_w):
        normed, norm_back = jax.vjp(rms_apply, stream, gain_vec)
        normed = normed.astype(jnp.bfloat16)
        gathered = spread(normed)
        gate_act = product(gathered, gate_w)
        up_act = product(gathered, up_w)
        hidden = (jax.nn.silu(gate_act) * up_act).astype(jnp.bfloat16)
        return (
            stream + collect(hidden, down_w),
            (norm_back, normed, gathered, gate_act, up_act, hidden),
        )

    def ffn_backward(stream_grad, kept_state, gate_w, up_w, down_w):
        norm_back, normed, gathered, gate_act, up_act, hidden = kept_state
        d_branch = spread_grad(stream_grad)
        d_hidden = right_product(d_branch, down_w)
        grad_down = left_product(hidden, d_branch)
        sigmoid_gate = jax.nn.sigmoid(gate_act)
        d_gate = (
            d_hidden * up_act * sigmoid_gate * (1.0 + gate_act * (1.0 - sigmoid_gate))
        ).astype(jnp.bfloat16)
        d_up = (d_hidden * gate_act * sigmoid_gate).astype(jnp.bfloat16)
        grad_gate = left_product(gathered, d_gate)
        grad_up = left_product(gathered, d_up)
        d_normed = collect_back(((d_gate, gate_w), (d_up, up_w)))
        d_stream, d_gain = norm_back(d_normed)
        return (stream_grad + d_stream, d_gain, [grad_gate, grad_up, grad_down])

    stream_zero = tokens.astype(jnp.float32)
    normed_mixer, norm_back_mixer = jax.vjp(rms_apply, stream_zero, gain_mixer)
    normed_mixer = normed_mixer.astype(jnp.bfloat16)
    gathered_mixer = spread(normed_mixer)
    mixer_x = product(gathered_mixer, mixer_in_x)
    gate_values = product(gathered_mixer, mixer_in_z)

    def conv_part(values, weight, bias_vec):
        return causal_conv(values, weight, bias_vec, documents)

    activated, conv_back = jax.vjp(conv_part, mixer_x, conv_weight, conv_bias)
    act_low = activated.astype(jnp.bfloat16)
    mixer_feats = lax.psum(product(act_low, mixer_proj), "mp")
    delta_low = mixer_feats[:, :RANK].astype(jnp.bfloat16)
    delta_pre = product(delta_low, delta_proj) + delta_bias[None, :]

    def scan_part(values, delta_in, input_map, output_map, decay_in, skip_in, gating):
        return selective_scan(
            values, delta_in, input_map, output_map, decay_in, skip_in, gating, carry_on
        )

    scanned, scan_back = jax.vjp(
        scan_part,
        activated,
        delta_pre,
        mixer_feats[:, RANK : RANK + STATE],
        mixer_feats[:, RANK + STATE :],
        decay_log,
        skip_weight,
        gate_values,
    )
    scanned_low = scanned.astype(jnp.bfloat16)
    stream_one = stream_zero + collect(scanned_low, mixer_out)
    stream_two, kept_first = ffn_forward(stream_one, gain_first, gate_first, up_first, down_first)
    normed_attn, norm_back_attn = jax.vjp(rms_apply, stream_two, gain_attn)
    normed_attn = normed_attn.astype(jnp.bfloat16)
    gathered_attn = spread(normed_attn)
    head_count = query_weight.shape[1] // HDIM
    queries = (
        product(gathered_attn, query_weight).astype(jnp.bfloat16).reshape(seq_len, head_count, HDIM)
    )
    key_rows = (
        product(gathered_attn, key_weight).astype(jnp.bfloat16).reshape(seq_len, head_count, HDIM)
    )
    value_rows = (
        product(gathered_attn, value_weight).astype(jnp.bfloat16).reshape(seq_len, head_count, HDIM)
    )
    attended, log_norm = attend_forward(queries, key_rows, value_rows, documents)
    attended_flat = attended.reshape(seq_len, head_count * HDIM)
    stream_three = stream_two + collect(attended_flat, output_weight)
    stream_four, kept_second = ffn_forward(
        stream_three, gain_second, gate_second, up_second, down_second
    )
    mixed_out = stream_four.astype(jnp.bfloat16)
    places = lax.axis_index("mp") * local_rows + jnp.arange(local_rows, dtype=jnp.int32)
    live_rows = (places < valid_len[0]).astype(jnp.float32)
    stream_grad = cotangent.astype(jnp.float32) * live_rows[:, None]
    stream_grad, d_gain_second, grads_second = ffn_backward(
        stream_grad, kept_second, gate_second, up_second, down_second
    )
    d_branch = spread_grad(stream_grad)
    d_attended = (
        right_product(d_branch, output_weight)
        .astype(jnp.bfloat16)
        .reshape(seq_len, head_count, HDIM)
    )
    grad_output = left_product(attended_flat, d_branch)
    d_queries, d_keys, d_values = attend_backward(
        queries, key_rows, value_rows, documents, log_norm, d_attended
    )
    d_queries = d_queries.reshape(seq_len, head_count * HDIM).astype(jnp.bfloat16)
    d_keys = d_keys.reshape(seq_len, head_count * HDIM).astype(jnp.bfloat16)
    d_values = d_values.reshape(seq_len, head_count * HDIM).astype(jnp.bfloat16)
    source = gathered_attn
    grads_attn = [
        left_product(source, d_queries),
        left_product(source, d_keys),
        left_product(source, d_values),
        grad_output,
    ]
    d_normed = collect_back(
        ((d_queries, query_weight), (d_keys, key_weight), (d_values, value_weight))
    )
    d_stream, d_gain_attn = norm_back_attn(d_normed)
    stream_grad = stream_grad + d_stream
    stream_grad, d_gain_first, grads_first = ffn_backward(
        stream_grad, kept_first, gate_first, up_first, down_first
    )
    d_branch = spread_grad(stream_grad)
    d_scanned = right_product(d_branch, mixer_out)
    grad_mixer_out = left_product(scanned_low, d_branch)
    d_act_scan, d_delta, d_in_map, d_out_map, grad_decay, grad_skip, d_gate_values = scan_back(
        d_scanned
    )
    d_delta_low = d_delta.astype(jnp.bfloat16)
    grad_delta_proj = left_product(delta_low, d_delta_low)
    grad_delta_bias = jnp.sum(d_delta_low.astype(jnp.float32), axis=0)
    d_feats = lax.psum(
        jnp.concatenate(
            [right_product(d_delta_low, delta_proj), d_in_map, d_out_map], axis=1
        ).astype(jnp.bfloat16),
        "mp",
    )
    grad_mixer_proj = left_product(act_low, d_feats)
    d_activated = d_act_scan + right_product(d_feats, mixer_proj)
    d_mixer_x, grad_conv_weight, grad_conv_bias = conv_back(d_activated)
    d_mixer_x = d_mixer_x.astype(jnp.bfloat16)
    d_gate_low = d_gate_values.astype(jnp.bfloat16)
    source = gathered_mixer
    grad_in_x = left_product(source, d_mixer_x)
    grad_in_z = left_product(source, d_gate_low)
    d_normed = collect_back(((d_mixer_x, mixer_in_x), (d_gate_low, mixer_in_z)))
    d_stream, d_gain_mixer = norm_back_mixer(d_normed)
    stream_grad = stream_grad + d_stream
    grads_mixer = [
        grad_in_x,
        grad_in_z,
        grad_conv_weight,
        grad_conv_bias,
        grad_mixer_proj,
        grad_delta_proj,
        grad_delta_bias,
        grad_decay,
        grad_skip,
        grad_mixer_out,
    ]
    joined = reduce_rows(grads_mixer + grads_first + grads_attn + grads_second)
    grads_mixer = joined[:10]
    grads_first = joined[10:13]
    grads_attn = joined[13:17]
    grads_second = joined[17:]
    gain_grads = lax.psum((d_gain_mixer, d_gain_first, d_gain_attn, d_gain_second), ("dp", "mp"))
    return (
        mixed_out,
        stream_grad,
        gain_grads[0],
        grads_mixer[0],
        grads_mixer[1],
        grads_mixer[2],
        grads_mixer[3],
        grads_mixer[4],
        grads_mixer[5],
        grads_mixer[6],
        grads_mixer[7],
        grads_mixer[8],
        grads_mixer[9],
        gain_grads[1],
        grads_first[0],
        grads_first[1],
        grads_first[2],
        gain_grads[2],
        grads_attn[0],
        grads_attn[1],
        grads_attn[2],
        grads_attn[3],
        gain_grads[3],
        grads_second[0],
        grads_second[1],
        grads_second[2],
    )


def solution(mesh):
    placed = (
        P(("dp", "mp"), None),
        P(("dp", "mp"), None),
        P("dp", None),
        P("dp"),
        P(),
        P(None, "mp"),
        P(None, "mp"),
        P(None, "mp"),
        P("mp"),
        P("mp", None),
        P(None, "mp"),
        P("mp"),
        P("mp", None),
        P("mp"),
        P("mp", None),
        P(),
        P(None, "mp"),
        P(None, "mp"),
        P("mp", None),
        P(),
        P(None, "mp"),
        P(None, "mp"),
        P(None, "mp"),
        P("mp", None),
        P(),
        P(None, "mp"),
        P(None, "mp"),
        P("mp", None),
    )
    return jax.shard_map(
        per_device,
        mesh=mesh,
        in_specs=placed,
        out_specs=(
            P(("dp", "mp"), None),
            P(("dp", "mp"), None),
            P(),
            P(None, "mp"),
            P(None, "mp"),
            P(None, "mp"),
            P("mp"),
            P("mp", None),
            P(None, "mp"),
            P("mp"),
            P("mp", None),
            P("mp"),
            P("mp", None),
            P(),
            P(None, "mp"),
            P(None, "mp"),
            P("mp", None),
            P(),
            P(None, "mp"),
            P(None, "mp"),
            P(None, "mp"),
            P("mp", None),
            P(),
            P(None, "mp"),
            P(None, "mp"),
            P("mp", None),
        ),
        check_vma=False,
    )
```

profile of v0, /device:TPU:0, one launch (start us, length us, event | category | flops | bytes accessed | tf_op | source)
XLA Modules:
  0.0 6148.7 jit_solution(2809464747686978909)
XLA Ops:
  42.1 31.5 all-reduce.99.cloned.1.call-done
  80.5 1052.9 %while.14 = (s32[]{:T(128)}, f32[768,16]{0,1:T(8,128)S(1)}, f32[32,16,768]{2,1,0:T(8,128)}, f32[32,768,16]{1,2,0:T(8,128)}, f32[32,16]{1,0:T(8,128)}, /*index=5*...) while((s32[]{:T(128)}, f32[768,16]{0,1:T(8,128)S(1)}, ...), condition=%wide.region_20.21_spmd.clone, body=%wide.region_3.20_spmd.clone.sunk | while | flops 1904658 | bytes 2121121 | solution.py:90
  1142.8 28.3 reduce-scatter.11.cloned.1.call-done
  1205.9 28.2 reduce-scatter.13.cloned.1.call-done
  1268.5 28.3 reduce-scatter.15.cloned.1.call-done
  1353.9 28.3 reduce-scatter.19.cloned.1.call-done
  1423.1 24.0 reduce-scatter.21.cloned.1.call-done
  1449.0 29.5 reduce-scatter.17.cloned.1.call-done
  1602.1 1968.7 %while.52 = (s32[]{:T(128)}, f32[768,16]{0,1:T(8,128)S(1)}, f32[768,16]{0,1:T(8,128)S(1)}, f32[32,16,768]{2,1,0:T(8,128)}, f32[32,16,768]{2,1,0:T(8,128)}, /*ind...) while((s32[]{:T(128)}, f32[768,16]{0,1:T(8,128)S(1)}, ...), condition=%wide.region_102.103_spmd.clone, body=%wide.region_37.102_spmd.clone.sunk | while | flops 8891396 | bytes 5687092 | solution.py:90
  3649.6 41.0 dynamic-update-slice.9
  3690.7 54.2 dynamic-update-slice.10
  3744.9 54.3 dynamic-update-slice.11
  3799.1 54.4 dynamic-update-slice.12
  3873.8 21.4 dynamic-update-slice.14
  3915.4 21.2 dynamic-update-slice.16
  3936.7 54.2 dynamic-update-slice.17
  3990.9 54.2 dynamic-update-slice.18
  4045.0 54.0 dynamic-update-slice.19
  4099.0 42.4 pad_bitcast_fusion
  4141.4 1211.2 %fusion = f32[15168,128]{1,0:T(8,128)} fusion(f32[121296,128]{1,0:T(8,128)} %pad_bitcast_fusion), kind=kCustom, calls=%all-reduce-scatter | all-reduce-scatter fusion | flops 15532033 | bytes 69870080
  5381.5 102.4 %all-reduce.95 = (f32[1536]{0:T(1024)}, f32[1536]{0:T(1024)}, f32[1536]{0:T(1024)}, f32[1536]{0:T(1024)}) all-reduce(f32[1536]{0:T(1024)S(1)} %get-tuple-element.815, f32[1536]{0:T(1024)S(1)} %copy-done.79, f32[1536]{0:T(1024)S(1)} %copy-done.78, f32[1536]{0:T(1024)S(1)} %copy-done.77), channel_id=1, replica_groups=mesh['dp'=8,'mp'=4] {'dp','mp'}, use_global_device_ids=true, to_apply=%region_107.108 | all-reduce | flops 6144 | bytes 49152 | tf_op jit(solution)/shard_map/psum | solution.py:427
  5486.3 495.3 %all-gather.27.cloned.1.call-done = bf16[8,15162,128]{2,1,0:T(8,128)(2,1)} async-done(((bf16[1,15162,128]{2,1,0:T(8,128)(2,1)}), bf16[8,15162,128]{2,1,0:T(8,128)(2,1)}) %all-gather.27.cloned.1.call-update) | async-done | bytes 31051792 | tf_op jit(solution)/shard_map/all_gather | solution.py:181
  5981.6 38.3 reshape.1581
  6035.0 25.3 fusion.143
  (4091 shorter events, 3592.5 us)
Async XLA Ops:
  7.2 1334.6 %copy-start = (bf16[1024,1536]{1,0:T(8,128)(2,1)S(1)}, bf16[1024,1536]{1,0:T(8,128)(2,1)}, u32[]{:S(2)}) copy-start(bf16[1024,1536]{1,0:T(8,128)(2,1)} %param.59) | copy-start | bytes 9437188
  7.3 25.8 all-gather.11.cloned.1.call-start
  10.6 63.0 %all-reduce.99.cloned.1.call-start = ((), (), s32[]{:S(2)}) async-start(), calls=%async_computation.9 | async-start | bytes 524288 | tf_op jit(solution)/shard_map/psum | solution.py:308
  41.4 1129.7 %reduce-scatter.11.cloned.1.call-start = ((), (), s32[]{:S(2)}) async-start(), calls=%async_computation.10 | async-start | bytes 1966080 | tf_op jit(solution)/shard_map/reduce_scatter | solution.py:244
  1142.8 51.5 all-gather.13.cloned.1.call-start
  1172.5 370.5 %copy-start.87 = (f32[128]{0:T(128)}, f32[128]{0:T(128)S(1)}, u32[]{:S(2)}) copy-start(f32[128]{0:T(128)S(1)} %fusion.131) | copy-start | bytes 1540
  1174.5 59.6 reduce-scatter.13.cloned.1.call-start
  1205.8 51.4 all-gather.15.cloned.1.call-start
  1237.4 59.3 reduce-scatter.15.cloned.1.call-start
  1268.4 51.6 all-gather.17.cloned.1.call-start
  1300.2 41.7 all-gather.19.cloned.1.call-start
  1302.1 80.0 %reduce-scatter.19.cloned.1.call-start = ((), (), s32[]{:S(2)}) async-start(), calls=%async_computation.18 | async-start | bytes 1966080 | tf_op jit(solution)/shard_map/reduce_scatter | solution.py:261
  1353.9 52.6 all-gather.21.cloned.1.call-start
  1386.7 60.4 reduce-scatter.21.cloned.1.call-start
  1418.8 59.6 reduce-scatter.17.cloned.1.call-start
  1423.0 77.8 %all-gather.23.cloned.1.call-start = ((), (), s32[]{:S(2)}) async-start(), calls=%async_computation.21 | async-start | bytes 1966080 | tf_op jit(solution)/shard_map/all_gather | solution.py:237
  1481.0 59.9 reduce-scatter.23.cloned.1.call-start
  1512.6 80.7 %all-gather.25.cloned.1.call-start = ((), (), s32[]{:S(2)}) async-start(), calls=%async_computation.23 | async-start | bytes 1966080 | tf_op jit(solution)/shard_map/all_gather | solution.py:237
  1545.1 2061.7 %all-reduce.101.cloned.1.call-start = ((), (), s32[]{:S(2)}) async-start(), calls=%async_computation.24 | async-start | bytes 262144 | tf_op jit(solution)/shard_map/psum | solution.py:393
  3575.2 1804.0 %reduce-scatter.25.cloned.1.call-start = ((), (), s32[]{:S(2)}) async-start(), calls=%async_computation.25 | async-start | bytes 1966080 | tf_op jit(solution)/shard_map/reduce_scatter | solution.py:261
  3619.6 2361.9 %all-gather.27.cloned.1.call-start = ((), (), s32[]{:S(2)}) async-start(), calls=%async_computation.26 | async-start | bytes 34947072 | tf_op jit(solution)/shard_map/all_gather | solution.py:181
  4141.4 1213.2 %copy-start.98 = (u32[32]{0:T(128)S(1)}, u32[32]{0:T(128)}, u32[]{:S(2)}) copy-start(u32[32]{0:T(128)} %constant.369) | copy-start | bytes 388
  5353.4 2.7 collective-permute-start
  5379.1 104.8 %copy-start.17 = (bf16[128,1536]{1,0:T(8,128)(2,1)S(1)}, bf16[128,1536]{1,0:T(8,128)(2,1)}, u32[]{:S(2)}) copy-start(bf16[128,1536]{1,0:T(8,128)(2,1)} %reduce-scatter.11.cloned.1.call-done) | copy-start | bytes 1179652
  (123 other events, 1669.9 us)
Sparse Core Ops, SparseCore 0:
  10.7 22.3 all-gather.10
  41.5 31.9 all-reduce.98
  1142.9 28.1 reduce-scatter.10
  1174.6 19.6 all-gather.12
  1205.9 28.1 reduce-scatter.12
  1237.5 19.6 all-gather.14
  1268.5 28.1 reduce-scatter.14
  1300.3 19.6 all-gather.16
  1322.1 19.6 all-gather.18
  1354.0 28.1 reduce-scatter.18
  1386.8 19.6 all-gather.20
  1418.9 28.1 reduce-scatter.20
  1450.2 28.1 reduce-scatter.16
  1481.2 19.6 all-gather.22
  1512.8 28.1 reduce-scatter.22
  1545.2 19.6 all-gather.24
  3575.3 31.3 all-reduce.100
  3619.7 28.1 reduce-scatter.24
  5379.3 602.1 all-gather.26
where the time goes:
time: 6230 us; the launch traced here: 6150 us
  other arithmetic  2400 us (39%)
  local copies, waits for them, and re-layouts  1420 us (23%)
  blocking collectives  1310 us (21%)
  waiting for transfers between devices  835 us (13%)
  matrix products  139 us (2%)
    unnamed x1, blocking collectives  1210 us
    reduce_sum x256, other arithmetic, one_block(): factor = jnp.exp(delta_block[position][:, None] * decay_rates)  931 us
    reduce_sum x160, other arithmetic, one_block(): jnp.sum(hidden_state * out_block[position][None, :], axis=1)  518 us
    all_gather x1, waiting for transfers between devices, reduce_rows(): lax.all_gather(lax.psum_scatter(grid_rows, 'dp', scatter_dimension=0, til...  495 us
    unnamed x280, local copies, waits for them, and re-layouts  473 us
    another operation x576, local copies, waits for them, and re-layouts, one_block(): return (hidden_state, jnp.stack(readouts))  355 us
    add_any x32, other arithmetic, selective_scan(): _, readouts = lax.scan(jax.checkpoint(one_block), initial, pieces)  336 us
    reduce_sum x32, other arithmetic, one_block(): hidden_state * out_block[position][None, :]  331 us

commit v1 on v0

v1 whole, which is shorter than its diff:
```python
import math

import jax
import jax.numpy as jnp
from jax import lax
from jax.experimental import pallas as pl
from jax.experimental.pallas import tpu as pltpu
from jax.sharding import PartitionSpec as P

STATE = 16
CONV = 4
RANK = 96
HDIM = 128
WINDOW = 2048

EPSILON = 1e-05
MASKED = -1e30
LOG2E = math.log2(math.e)
STEP = 16
BLOCK = 64
LANES = 128
RESET = 1e30
f32 = jnp.float32
bf16 = jnp.bfloat16
MIB = 1024 * 1024


def product(left_rows, weight, kind=f32):
    return jnp.dot(left_rows, weight, preferred_element_type=f32).astype(kind)


def left_product(left_rows, right_rows, kind=f32):
    return lax.dot_general(
        left_rows, right_rows, (((0,), (0,)), ((), ())), preferred_element_type=f32
    ).astype(kind)


def right_product(left_rows, weight, kind=f32):
    return lax.dot_general(
        left_rows, weight, (((1,), (1,)), ((), ())), preferred_element_type=f32
    ).astype(kind)


def rms_apply(stream, gain_vec):
    return (
        stream * lax.rsqrt(jnp.mean(stream * stream, axis=-1, keepdims=True) + EPSILON) * gain_vec
    )


def document_ids(starts, length, seq_len):
    places = jnp.arange(seq_len, dtype=jnp.int32)
    counted = jnp.sum((starts[None, :] <= places[:, None]).astype(jnp.int32), axis=1) - 1
    return jnp.where(places < length, counted, starts.shape[0])


def causal_conv(mixer_x, conv_weight, conv_bias, documents):
    running_sum = conv_bias[None, :] + conv_weight[0][None, :] * mixer_x
    for lag_steps in range(1, CONV):
        shifted = jnp.concatenate(
            [jnp.zeros((lag_steps, mixer_x.shape[1]), mixer_x.dtype), mixer_x[:-lag_steps]], axis=0
        )
        before = jnp.concatenate([jnp.full((lag_steps,), -1, jnp.int32), documents[:-lag_steps]])
        same_doc = (before == documents).astype(mixer_x.dtype)
        running_sum = running_sum + conv_weight[lag_steps][None, :] * shifted * same_doc[:, None]
    return jax.nn.silu(running_sum)


def softplus(v):
    return jnp.maximum(v, 0.0) + jnp.log1p(jnp.exp(-jnp.abs(v)))

def lane_fold(v):
    total = v[:, :128]
    for j in range(1, v.shape[1] // 128):
        total = total + v[:, 128 * j:128 * (j + 1)]
    return total

def scan_fwd_kernel(act_ref, pre_ref, gate_ref, keep_ref, b_ref, c_ref, rate_ref, skip_ref,
                    out_ref, res_ref, hs_ref, h_ref, dk_ref, u_ref):
    @pl.when(pl.program_id(0) == 0)
    def _():
        h_ref[...] = jnp.zeros_like(h_ref)
    tb = act_ref.shape[0]
    delta = softplus(pre_ref[...])
    dk_ref[...] = jnp.where(keep_ref[...][:, :1] > 0.0, delta, RESET)
    u_ref[...] = delta * act_ref[...]
    rate2 = rate_ref[...] * LOG2E
    lanes = act_ref.shape[1]

    def body(k, h):
        base = pl.multiple_of(k * STEP, STEP)
        rows = []
        for i in range(STEP):
            dk = dk_ref[pl.ds(base + i, 1), :]
            u = u_ref[pl.ds(base + i, 1), :]
            bt = jnp.concatenate([b_ref[base + i]] * (lanes // 128), axis=1)
            ct = jnp.concatenate([c_ref[base + i]] * (lanes // 128), axis=1)
            h = jnp.exp2(dk * rate2) * h + u * bt
            hs_ref[base + i] = h.astype(hs_ref.dtype)
            rows.append(jnp.sum(h * ct, axis=0, keepdims=True))
        read = jnp.concatenate(rows, axis=0)
        res = read + skip_ref[...] * act_ref[pl.ds(base, STEP), :]
        res_ref[pl.ds(base, STEP), :] = res
        g = gate_ref[pl.ds(base, STEP), :]
        out_ref[pl.ds(base, STEP), :] = (res * g * jax.nn.sigmoid(g)).astype(out_ref.dtype)
        return h

    h_ref[...] = lax.fori_loop(0, tb // STEP, body, h_ref[...])


def scan_fwd(act, pre, gate, keep_b, b_b, c_b, rate_t, skip, tb=BLOCK, hs_dtype=f32):
    t, c = act.shape
    n = rate_t.shape[0]
    tb = min(tb, t)
    row = pl.BlockSpec((tb, c), lambda i: (i, 0))
    return pl.pallas_call(
        scan_fwd_kernel,
        grid=(t // tb,),
        in_specs=[row, row, row, pl.BlockSpec((tb, 128), lambda i: (i, 0)),
                  pl.BlockSpec((tb, n, 128), lambda i: (i, 0, 0)),
                  pl.BlockSpec((tb, n, 128), lambda i: (i, 0, 0)),
                  pl.BlockSpec((n, c), lambda i: (0, 0)),
                  pl.BlockSpec((1, c), lambda i: (0, 0))],
        out_specs=[row, row, pl.BlockSpec((tb, n, c), lambda i: (i, 0, 0))],
        out_shape=[jax.ShapeDtypeStruct((t, c), bf16),
                   jax.ShapeDtypeStruct((t, c), f32),
                   jax.ShapeDtypeStruct((t, n, c), hs_dtype)],
        scratch_shapes=[pltpu.VMEM((n, c), f32), pltpu.VMEM((tb, c), f32),
                        pltpu.VMEM((tb, c), f32)],
        compiler_params=pltpu.CompilerParams(vmem_limit_bytes=20 * MIB),
        cost_estimate=pl.CostEstimate(flops=t * c * n * 40, bytes_accessed=t * c * 100, transcendentals=t * c * n),
        name="scan_forward",
    )(act, pre, gate, keep_b, b_b, c_b, rate_t, skip)


def scan_bwd_kernel(carried, act_ref, pre_ref, gate_ref, res_ref, ds_ref, keep_ref, b_ref, c_ref,
                    rate_ref, skip_ref, hs_ref, hp_ref, *refs):
    if carried:
        before, refs = refs[:9], refs[9:]
    (dact_ref, dpre_ref, dgate_ref, db_ref, dc_ref, drate_ref, dskip_ref, dbias_ref, g_ref,
     dk_ref, u_ref, dl_ref, dy_ref, wide_b_ref, wide_c_ref) = refs

    @pl.when(pl.program_id(0) == 0)
    def _():
        for n, ref in ((5, drate_ref), (6, dskip_ref), (7, dbias_ref), (8, g_ref)):
            ref[...] = before[n][...] if carried else jnp.zeros_like(ref)

    tb = act_ref.shape[0]
    lanes = act_ref.shape[1]
    delta = softplus(pre_ref[...])
    dl_ref[...] = delta
    dk_ref[...] = jnp.where(keep_ref[...][:, :1] > 0.0, delta, RESET)
    u_ref[...] = delta * act_ref[...]
    gate = gate_ref[...]
    sg = jax.nn.sigmoid(gate)
    ds = ds_ref[...]
    dgate_ref[...] = (ds * res_ref[...] * sg * (1.0 + gate * (1.0 - sg))).astype(dgate_ref.dtype)
    dy = ds * gate * sg
    dy_ref[...] = dy
    dskip_ref[...] += jnp.sum(dy * act_ref[...], axis=0, keepdims=True)
    rate = rate_ref[...]
    rate2 = rate * LOG2E
    nk = tb // STEP

    def body(kk, carry):
        g, drate = carry
        k = nk - 1 - kk
        base = pl.multiple_of(k * STEP, STEP)
        r1s = [None] * STEP
        r2s = [None] * STEP
        h = hs_ref[base + STEP - 1]
        for i in range(STEP - 1, -1, -1):
            dk = dk_ref[pl.ds(base + i, 1), :]
            u = u_ref[pl.ds(base + i, 1), :]
            dyr = dy_ref[pl.ds(base + i, 1), :]
            dl = dl_ref[pl.ds(base + i, 1), :]
            bt = jnp.concatenate([b_ref[base + i]] * (lanes // 128), axis=1)
            ct = jnp.concatenate([c_ref[base + i]] * (lanes // 128), axis=1)
            wide_c_ref[base + i] = lane_fold(h * dyr)
            if i > 0:
                hprev = hs_ref[base + i - 1]
            else:
                inside = hs_ref[jnp.maximum(base - 1, 0)]
                hprev = jnp.where(base > 0, inside, hp_ref[hp_ref.shape[0] - 1])
            lam = g + ct * dyr
            wide_b_ref[base + i] = lane_fold(lam * u)
            r2s[i] = jnp.sum(lam * bt, axis=0, keepdims=True)
            g = jnp.exp2(dk * rate2) * lam
            w = g * hprev
            drate = drate + w * dl
            r1s[i] = jnp.sum(w * rate, axis=0, keepdims=True)
            h = hprev
        r1 = jnp.concatenate(r1s, axis=0)
        r2 = jnp.concatenate(r2s, axis=0)
        sl = pl.ds(base, STEP)
        a = act_ref[sl, :]
        d_delta = r1 + a * r2
        dpre = (d_delta * jax.nn.sigmoid(pre_ref[sl, :])).astype(bf16)
        dpre_ref[sl, :] = dpre
        dact_ref[sl, :] = dl_ref[sl, :] * r2 + skip_ref[...] * dy_ref[sl, :]
        dbias_ref[...] += jnp.sum(dpre.astype(f32), axis=0, keepdims=True)
        return (g, drate)

    g, drate = lax.fori_loop(0, nk, body, (g_ref[...], jnp.zeros_like(g_ref)))
    g_ref[...] = g
    drate_ref[...] += drate
    db_ref[...] = jnp.sum(wide_b_ref[...], axis=2)
    dc_ref[...] = jnp.sum(wide_c_ref[...], axis=2)


def scan_bwd(act, pre, gate, res, ds, keep_b, b_b, c_b, rate_t, skip, hs, before=None, tb=BLOCK):
    t, c = act.shape
    n = rate_t.shape[0]
    nb = t // tb
    steps = nb // 2
    top = nb - 1 if before is None else steps - 1
    row = pl.BlockSpec((tb, c), lambda i: (top - i, 0))
    one = pl.BlockSpec((1, c), lambda i: (0, 0))
    state = pl.BlockSpec((n, c), lambda i: (0, 0))
    bl = pl.BlockSpec((tb, n, 128), lambda i: (top - i, 0, 0))
    maps = pl.BlockSpec((tb, n), lambda i: (top - i, 0))
    per = tb // 8
    shapes = [
        ((t, c), f32), ((t, c), bf16), ((t, c), bf16), ((t, n), f32), ((t, n), f32),
        ((n, c), f32), ((1, c), f32), ((1, c), f32), ((n, c), f32),
    ]
    held = pl.BlockSpec(memory_space=pltpu.HBM)
    carried = before is not None
    return pl.pallas_call(
        lambda *refs: scan_bwd_kernel(carried, *refs),
        grid=(steps,),
        in_specs=[row, row, row, row, row, pl.BlockSpec((tb, 128), lambda i: (top - i, 0)),
                  bl, bl, state, one,
                  pl.BlockSpec((tb, n, c), lambda i: (top - i, 0, 0)),
                  pl.BlockSpec((8, n, c), lambda i: (jnp.maximum((top - i) * per - 1, 0), 0, 0))]
        + ([held] * 5 + [state, one, one, state] if carried else []),
        out_specs=[row, row, row, maps, maps, state, one, one, state],
        out_shape=[jax.ShapeDtypeStruct(*shape) for shape in shapes],
        input_output_aliases={12 + k: k for k in range(5)} if carried else {},
        scratch_shapes=[pltpu.VMEM((tb, c), f32)] * 4 + [pltpu.VMEM((tb, n, 128), f32)] * 2,
        compiler_params=pltpu.CompilerParams(vmem_limit_bytes=28 * MIB),
        cost_estimate=pl.CostEstimate(flops=t * c * n * 100, bytes_accessed=t * c * 100, transcendentals=t * c * n),
        name="scan_backward",
    )(act, pre, gate, res, ds, keep_b, b_b, c_b, rate_t, skip, hs, hs, *(before or ()))


def visible(docs_row_ref, docs_col_ref):
    seq_len = docs_row_ref.shape[1]
    row_pos = lax.broadcasted_iota(jnp.int32, (seq_len, seq_len), 0)
    places = lax.broadcasted_iota(jnp.int32, (seq_len, seq_len), 1)
    same = docs_row_ref[0:1, :] == docs_col_ref[:, 0:1]
    return (places <= row_pos) & (row_pos - places < WINDOW) & same


def probabilities(queries, key_rows, allowed):
    scores = right_product(queries, key_rows) * HDIM ** (-0.5)
    scores = jnp.where(allowed, scores, MASKED)
    weights = jnp.exp(scores - jnp.max(scores, axis=-1, keepdims=True))
    return weights / jnp.sum(weights, axis=-1, keepdims=True)


def attend_forward_kernel(q_ref, k_ref, v_ref, docs_row_ref, docs_col_ref, out_ref):
    allowed = visible(docs_row_ref, docs_col_ref)
    for start in range(0, q_ref.shape[1], HDIM):
        head = slice(start, start + HDIM)
        probs = probabilities(q_ref[:, head], k_ref[:, head], allowed).astype(bf16)
        out_ref[:, head] = product(probs, v_ref[:, head], bf16)


def attend_backward_kernel(q_ref, k_ref, v_ref, d_ref, docs_row_ref, docs_col_ref, out_ref):
    allowed = visible(docs_row_ref, docs_col_ref)
    width = q_ref.shape[1]
    score_scale = HDIM ** (-0.5)
    for start in range(0, width, HDIM):
        head = slice(start, start + HDIM)
        queries, key_rows, d_out = q_ref[:, head], k_ref[:, head], d_ref[:, head]
        probs = probabilities(queries, key_rows, allowed)
        d_probs = right_product(d_out, v_ref[:, head])
        inner = jnp.sum(probs * d_probs, axis=-1, keepdims=True)
        d_scores = (probs * (d_probs - inner)).astype(bf16)
        out_ref[:, head] = (product(d_scores, key_rows) * score_scale).astype(bf16)
        out_ref[:, width + start : width + start + HDIM] = (
            left_product(d_scores, queries) * score_scale
        ).astype(bf16)
        out_ref[:, 2 * width + start : 2 * width + start + HDIM] = left_product(
            probs.astype(bf16), d_out, bf16
        )


def attend(kernel, operands, documents, columns, name):
    seq_len, width = operands[0].shape
    docs_row = jnp.broadcast_to(documents[None, :], (8, seq_len))
    docs_col = jnp.broadcast_to(documents[:, None], (seq_len, LANES))
    return pl.pallas_call(
        kernel,
        out_shape=jax.ShapeDtypeStruct((seq_len, columns), bf16),
        compiler_params=pltpu.CompilerParams(vmem_limit_bytes=24 * MIB),
        cost_estimate=pl.CostEstimate(
            flops=10 * seq_len * seq_len * width,
            bytes_accessed=16 * seq_len * width,
            transcendentals=seq_len * seq_len * width // HDIM,
        ),
        name=name,
    )(*operands, docs_row, docs_col)


def core_swap(v):
    return lax.ppermute(v, "mp", [(0, 1), (1, 0), (2, 3), (3, 2)])


def chip_swap(v):
    return lax.ppermute(v, "mp", [(0, 2), (2, 0), (1, 3), (3, 1)])


def sum_mp(v):
    v = v + core_swap(v)
    return v + chip_swap(v)


def dp_permute(v, pairs):
    return lax.ppermute(v, "dp", pairs)


X_SWAP = [(i, i ^ 1) for i in range(8)]
Z_MID = [(2, 4), (4, 2), (3, 5), (5, 3)]
Z_NEAR = [(0, 2), (2, 0), (1, 3), (3, 1), (4, 6), (6, 4), (5, 7), (7, 5)]
Z_FAR = [(0, 4), (4, 0), (1, 5), (5, 1), (2, 6), (6, 2), (3, 7), (7, 3)]
TAIL = (192,)
PAIRS = {"x": X_SWAP, "near": Z_NEAR, "mid": Z_MID}


def sum_dp_small(v):
    if lax.axis_size("dp") != 8:
        return lax.psum(v, "dp")
    v = v + dp_permute(v, X_SWAP)
    v = v + dp_permute(v, Z_NEAR)
    return v + dp_permute(v, Z_FAR)


def widen(v):
    return v.astype(f32)


def add_low(left, right):
    return (widen(left) + widen(right)).astype(bf16)


def pack(grad):
    rows, columns = grad.shape
    groups = grad.reshape(rows, columns // LANES, LANES)
    return jnp.transpose(groups, (1, 0, 2)).reshape(rows * columns // LANES, LANES)


def grad_kernel(slabs, left_ref, right_ref, *refs):
    out_ref = refs[-1]
    rows = left_ref.shape[1]
    total = left_product(left_ref[...], right_ref[...])
    for j in range(slabs):
        out_ref[j * rows : (j + 1) * rows] = total[:, j * LANES : (j + 1) * LANES].astype(bf16)


def packed_grad(left_rows, right_rows, total_rows=None, at=0, into=None):
    tokens_here, rows = left_rows.shape
    groups = right_rows.shape[1] // LANES
    slabs = 4 if groups % 4 == 0 else 3
    if total_rows is None:
        total_rows = groups * rows
    specs = [
        pl.BlockSpec((tokens_here, rows), lambda i: (0, 0)),
        pl.BlockSpec((tokens_here, slabs * LANES), lambda i: (0, i)),
    ]
    operands = [left_rows, right_rows]
    aliases = {}
    if into is not None:
        specs.append(pl.BlockSpec(memory_space=pltpu.HBM))
        operands.append(into)
        aliases = {2: 0}
    first = at // (slabs * rows)
    return pl.pallas_call(
        lambda *refs: grad_kernel(slabs, *refs),
        grid=(groups // slabs,),
        in_specs=specs,
        out_specs=pl.BlockSpec((slabs * rows, LANES), lambda i: (first + i, 0)),
        out_shape=jax.ShapeDtypeStruct((total_rows, LANES), bf16),
        input_output_aliases=aliases,
        compiler_params=pltpu.CompilerParams(vmem_limit_bytes=20 * MIB),
        cost_estimate=pl.CostEstimate(
            flops=2 * tokens_here * rows * groups * LANES,
            bytes_accessed=4 * rows * groups * LANES,
            transcendentals=0,
        ),
        name="weight_grad",
    )(*operands)


def unpack(packed, rows):
    groups = packed.reshape(packed.shape[0] // rows, rows, LANES)
    return widen(jnp.transpose(groups, (1, 0, 2)).reshape(rows, -1))


SENDS = {
    "x": (("x1", 0, 2), ("zx", 2, 2), ("xf", 5, 2)),
    "in": (("xi", 1, 2), ("zi", 0, 4)),
    "mid": (("zm", 1, 2), ("xm", 2, 1), ("xn", 3, 1), ("zn", 3, 2)),
    "out": (("xo", 4, 2), ("zo", 4, 4)),
    "held": (("h", 1, 2), ("sz", 1, 2), ("sx", 2, 1)),
}


def layout(chunks):
    found = {}
    for channel, parts in SENDS.items():
        at, spots = 0, {}
        for name, stage, count in parts:
            if stage in chunks:
                spots[name] = (at, chunks[stage], count)
                at += chunks[stage] * count
        if at:
            found[channel] = (spots, at)
    into, out = found.pop("in", ({}, 0)), found.pop("out", ({}, 0))
    if into[1] or out[1]:
        found["near"] = ({**into[0], **out[0]}, max(into[1], out[1]), into[1] != out[1])
    return found


def chunk_rows(first, chunk, at, count):
    if isinstance(at, int):
        return pl.ds(first + at * chunk, count * chunk)
    return pl.ds(pl.multiple_of(first + at * chunk, 16), count * chunk)


def round_kernel(chunks, in_names, out_names, before, after, at0, at1, flags_ref, *refs):
    ins = dict(zip(in_names, refs[: len(in_names)]))
    refs = refs[len(in_names) :]
    outs = dict(zip(out_names, refs[: len(out_names)]))
    refs = refs[len(out_names) :]
    own_ref, sems = refs
    x, high, middle = flags_ref[0], flags_ref[1], flags_ref[2]
    low, outer = 1 - high, 1 - middle

    def part(spots, ref, name, at, count):
        first, chunk, whole = spots[0][name]
        return ref.at[chunk_rows(first, chunk, at, whole if count is None else count)]

    def came(channel, name, prefix, at=0, count=None):
        return part(before[channel], ins[prefix + channel], name, at, count)

    def goes(channel, name, at=0, count=None):
        return part(after[channel], outs[channel], name, at, count)

    def got(*spot):
        return came(*spot)[...]

    def put(channel, name, value):
        goes(channel, name)[...] = value

    def put_joined(channel, name, mine, other, second):
        half = after[channel][0][name][2] // 2
        goes(channel, name, second * half, half)[...] = mine
        goes(channel, name, (1 - second) * half, half)[...] = other

    copies = []

    def copy(source, target, when=None):
        move = pltpu.make_async_copy(source, target, sems.at[len(copies)])
        copies.append((move, when))
        if when is None:
            move.start()
        else:
            pl.when(when == 1)(move.start)
        return move

    def finish(move, when):
        if when is None:
            move.wait()
        else:
            pl.when(when == 1)(move.wait)

    if 1 in chunks:
        c = chunks[1]
        one = copy(ins["g1"].at[chunk_rows(at1, c, 2 * x, 2)], own_ref.at[chunk_rows(0, c, 0, 2)])
        two = copy(ins["g1"].at[chunk_rows(at1, c, 4, 4)], own_ref.at[chunk_rows(0, c, 2, 4)])
    if "near" in outs and after["near"][2]:
        outs["near"][...] = jnp.zeros_like(outs["near"])
    if 0 in chunks:
        c = chunks[0]
        copy(ins["g0"].at[chunk_rows(at0, c, 2 * (1 - x), 2)], goes("x", "x1"))
        copy(ins["g0"].at[chunk_rows(at0, c, 4, 4)], goes("near", "zi"), outer)
    if 5 in chunks:
        copy(came("near", "zo", "p_"), outs["fz"], middle)
        copy(came("near", "zo", "r_"), outs["fz"], outer)
    if 6 in chunks:
        c = chunks[6]
        copy(came("x", "xf", "p_"), outs["fx"].at[chunk_rows(0, c, 2 * x, 2)])
        copy(came("x", "xf", "r_"), outs["fx"].at[chunk_rows(0, c, 2 * (1 - x), 2)])
    if 2 in chunks:
        put("mid", "xm", add_low(got("held", "h", "p_", low, 1), got("near", "xi", "r_", low, 1)))
        put("held", "sx", add_low(got("held", "h", "p_", high, 1), got("near", "xi", "r_", high, 1)))
        put("x", "zx", add_low(got("held", "sz", "p_"), got("mid", "zm", "r_")))
    if 3 in chunks:
        put("mid", "xn", add_low(got("held", "sx", "p_"), got("mid", "xm", "r_")))
        put("mid", "zn", add_low(got("x", "zx", "p_"), got("x", "zx", "r_")))
    if 4 in chunks:

        @pl.when(middle == 1)
        def _():
            put_joined("near", "xo", got("mid", "xn", "p_"), got("mid", "xn", "r_"), high)
            put_joined("near", "zo", got("mid", "zn", "p_"), got("mid", "zn", "r_"), high)

    if 5 in chunks:

        @pl.when(middle == 1)
        def _():
            put("x", "xf", got("near", "xo", "p_"))

        @pl.when(middle == 0)
        def _():
            put("x", "xf", got("near", "xo", "r_"))

    if 1 in chunks:
        c = chunks[1]
        one.wait()
        two.wait()
        own = add_low(own_ref[chunk_rows(0, c, 0, 2)], got("x", "x1", "r_"))
        put("held", "h", own)

        @pl.when(middle == 0)
        def _():
            put("near", "xi", own)

        away, mine = 2 * low, 2 * high
        put(
            "mid",
            "zm",
            add_low(own_ref[chunk_rows(0, c, 2 + away, 2)], got("near", "zi", "r_", away, 2)),
        )
        put(
            "held",
            "sz",
            add_low(own_ref[chunk_rows(0, c, 2 + mine, 2)], got("near", "zi", "r_", mine, 2)),
        )
    for move, when in copies[2 if 1 in chunks else 0 :]:
        finish(move, when)


NEEDS = {
    0: (),
    1: ("r_x", "r_near"),
    2: ("p_held", "r_near", "r_mid"),
    3: ("p_held", "r_mid", "p_x", "r_x"),
    4: ("p_mid", "r_mid"),
    5: ("p_near", "r_near"),
    6: ("p_x", "r_x"),
}


class RowSums:
    def __init__(self):
        place = lax.axis_index("dp")
        x, z = place % 2, place // 2
        high = (z >= 2).astype(jnp.int32)
        middle = ((z == 1) | (z == 2)).astype(jnp.int32)
        self.flags = jnp.stack([x.astype(jnp.int32), high, middle])
        self.flying = {}
        self.values = {}
        self.spots = {}
        self.sizes = {}
        self.done = {}
        self.last = None
        self.whole = lax.axis_size("dp") == 8

    def round(self, key, source, chain):
        if not self.whole:
            if key is not None:
                array, first, size = source
                total = lax.psum(array[first : first + 8 * size], "dp")
                self.done[key] = [total[: 4 * size], total[4 * size :]]
            return chain
        moved = {stage + 1: name for stage, name in self.flying.items()}
        if key is not None:
            moved[0] = key
            self.sizes[key] = source[2]
        self.flying = {stage: name for stage, name in moved.items() if stage < 6}
        stages = {stage: self.sizes[name] for stage, name in sorted(moved.items())}
        before, after = self.spots, layout(stages)
        wanted = sorted({name for stage in stages for name in NEEDS[stage]})
        in_hbm = pl.BlockSpec(memory_space=pltpu.HBM)
        in_vmem = pl.BlockSpec(memory_space=pltpu.VMEM)
        operands, specs, in_names = [], [], []
        at0 = at1 = 0
        if 0 in moved:
            in_names.append("g0")
            operands.append(source[0])
            specs.append(in_hbm)
            at0 = source[1]
        if 1 in moved:
            in_names.append("g1")
            operands.append(self.last[0])
            specs.append(in_hbm)
            at1 = self.last[1]
        for name in wanted:
            in_names.append(name)
            operands.append(self.values[name])
            specs.append(in_vmem)
        out_names = list(after)
        counts = [after[name][1] for name in out_names]
        out_specs = [in_vmem] * len(counts)
        for stage, name in ((5, "fz"), (6, "fx")):
            if stage in moved:
                out_names.append(name)
                counts.append(4 * stages[stage])
                out_specs.append(in_hbm)
        touched = 80 * LANES * max(stages.values())

        def body(*refs):
            round_kernel(stages, in_names, out_names, before, after, at0, at1, *refs)

        results = pl.pallas_call(
            body,
            in_specs=[pl.BlockSpec(memory_space=pltpu.SMEM)] + specs,
            out_specs=out_specs,
            out_shape=[jax.ShapeDtypeStruct((count, LANES), bf16) for count in counts],
            scratch_shapes=[
                pltpu.VMEM((6 * stages.get(1, 16), LANES), bf16),
                pltpu.SemaphoreType.DMA((8,)),
            ],
            compiler_params=pltpu.CompilerParams(vmem_limit_bytes=6 * MIB),
            cost_estimate=pl.CostEstimate(
                flops=touched, bytes_accessed=touched, transcendentals=0
            ),
            name="round",
        )(self.flags, *operands)
        results = dict(zip(out_names, results))
        if 5 in moved:
            self.done[moved[5]] = [results.pop("fz")]
        if 6 in moved:
            self.done[moved[6]].insert(0, results.pop("fx"))
        if 0 in moved:
            self.last = source
        self.spots = after
        if chain is not None:
            chain = lax.optimization_barrier((results, chain))[1]
        self.values = {"p_" + name: value for name, value in results.items()}
        for channel, pairs in PAIRS.items():
            if channel in results:
                self.values["r_" + channel] = dp_permute(results[channel], pairs)
        return chain


def buckets(name, packed, sizes):
    found, at = [], 0
    while at < packed.shape[0]:
        size = sizes[min(len(found), len(sizes) - 1)]
        found.append(((name, len(found)), (packed, at, size)))
        at += 8 * size
    assert at == packed.shape[0]
    return found


def unpack_kernel(starts, *refs):
    out_ref = refs[-1]
    step = pl.program_id(0)
    for number, ref in enumerate(refs[:-1]):

        @pl.when((starts[number] <= step) & (step < starts[number + 1]))
        def _(ref=ref):
            out_ref[...] = widen(ref[...])


def unpack_parts(parts, rows, start=0, length=None):
    if length is not None:
        at, kept = 0, []
        for part in parts:
            if start <= at < start + length:
                kept.append(part)
            at += part.shape[0]
        parts = kept
    piece = math.gcd(rows, *[part.shape[0] for part in parts])
    starts = [0]
    for part in parts:
        starts.append(starts[-1] + part.shape[0] // piece)
    steps, per_group = starts[-1], rows // piece
    columns = steps // per_group * LANES

    def spec(first, last):
        return pl.BlockSpec((piece, LANES), lambda i: (jnp.clip(i - first, 0, last - first - 1), 0))

    return pl.pallas_call(
        lambda *refs: unpack_kernel(starts, *refs),
        grid=(steps,),
        in_specs=[spec(starts[n], starts[n + 1]) for n in range(len(parts))],
        out_specs=pl.BlockSpec((piece, LANES), lambda i: (i % per_group, i // per_group)),
        out_shape=jax.ShapeDtypeStruct((rows, columns), f32),
        compiler_params=pltpu.CompilerParams(vmem_limit_bytes=12 * MIB),
        cost_estimate=pl.CostEstimate(
            flops=rows * columns, bytes_accessed=6 * rows * columns, transcendentals=0
        ),
        name="unpack",
    )(*parts)


def per_device(
    tokens,
    cotangent,
    doc_starts,
    valid_len,
    gain_mixer,
    mixer_in_x,
    mixer_in_z,
    conv_weight,
    conv_bias,
    mixer_proj,
    delta_proj,
    delta_bias,
    decay_log,
    skip_weight,
    mixer_out,
    gain_first,
    gate_first,
    up_first,
    down_first,
    gain_attn,
    query_weight,
    key_weight,
    value_weight,
    output_weight,
    gain_second,
    gate_second,
    up_second,
    down_second,
):
    local_rows, width = tokens.shape
    seq_len = local_rows * 4
    place = lax.axis_index("mp")
    chip, core = place // 2, place % 2
    documents = document_ids(doc_starts[0], valid_len[0], seq_len)
    before = jnp.concatenate([jnp.full((1,), -1, jnp.int32), documents[:-1]])
    carry_on = (before == documents).astype(f32)
    places = jnp.arange(seq_len, dtype=jnp.int32)
    def both_halves(mine):
        other = chip_swap(mine)
        return jnp.stack([jnp.where(chip == 0, mine, other), jnp.where(chip == 0, other, mine)])

    def spread(mine):
        other = core_swap(mine)
        joined = jnp.stack(
            [jnp.where(core == 0, mine, other), jnp.where(core == 0, other, mine)], axis=1
        )
        return joined.reshape(seq_len, width)

    def half_rows(rows, which):
        cut = rows.reshape(2, 2, local_rows, rows.shape[1])
        return lax.dynamic_index_in_dim(cut, which, 1, keepdims=False).reshape(
            2 * local_rows, rows.shape[1]
        )

    def collect(pairs, multiply):
        away = multiply(half_rows(pairs[0][0], 1 - core), pairs[0][1])
        mine = multiply(half_rows(pairs[0][0], core), pairs[0][1])
        for rows, weight in pairs[1:]:
            away = away + multiply(half_rows(rows, 1 - core), weight)
            mine = mine + multiply(half_rows(rows, core), weight)
        mine = mine + widen(core_swap(away.astype(bf16)))
        mine = mine + widen(chip_swap(mine.astype(bf16)))
        return mine.reshape(2, local_rows, width)

    def ffn_forward(stream, gain_vec, gate_w, up_w, down_w):
        gathered = spread(rms_apply(stream, gain_vec).astype(bf16))
        gate_act = product(gathered, gate_w)
        up_act = product(gathered, up_w)
        hidden = (jax.nn.silu(gate_act) * up_act).astype(bf16)
        return (
            stream + collect(((hidden, down_w),), product),
            (stream, gathered, gate_act, up_act, hidden),
        )

    def ffn_pointwise(d_hidden, kept_state):
        _, _, gate_act, up_act, _ = kept_state
        sigmoid_gate = jax.nn.sigmoid(gate_act)
        d_gate = (
            d_hidden * up_act * sigmoid_gate * (1.0 + gate_act * (1.0 - sigmoid_gate))
        ).astype(bf16)
        return d_gate, (d_hidden * gate_act * sigmoid_gate).astype(bf16)

    def norm_backward(stream_grad, stream, gain_vec, d_normed):
        d_stream, d_gain = jax.vjp(rms_apply, stream, gain_vec)[1](d_normed)
        return stream_grad + d_stream, d_gain

    streams = [RowSums(), RowSums()]
    chunk = width // 4
    queue = []
    turn = [0]
    wanted = {}
    found = {}
    fresh = []

    def push(name, packed, rows, sizes=(chunk,)):
        parts = buckets(name, packed, sizes)
        wanted[name] = (rows, [key for key, _ in parts])
        queue.extend(parts)

    def unpack_finished(limit):
        done = {}
        for stream in streams:
            done.update(stream.done)
        for name, (rows, keys) in list(wanted.items()):
            if limit and all(len(done.get(key, ())) == 2 for key in keys):
                limit -= 1
                parts = [part for key in keys for part in done[key]]
                del wanted[name]
                if rows:
                    found[name] = unpack_parts(parts, rows)
                    fresh.append(name)
                else:
                    pieces = heads_width * width // LANES
                    for n, head_name in enumerate(("query", "key", "value")):
                        found[head_name] = unpack_parts(parts, width, n * pieces, pieces)
                        fresh.append(head_name)
                    found["output"] = unpack_parts(parts, heads_width, 3 * pieces, pieces)
                    fresh.append("output")

    def tick(chain=()):
        stream = streams[turn[0] % 2]
        turn[0] += 1
        if not queue and not stream.flying:
            return chain
        key, source = queue.pop(0) if queue else (None, None)
        names = list(fresh)
        fresh.clear()
        ready, chain = stream.round(key, source, ([found[name] for name in names], chain))
        found.update(zip(names, ready))
        unpack_finished(1)
        return chain

    def collect_back(grads, weights):
        if isinstance(grads, tuple):
            away = [half_rows(rows, 1 - core) for rows in grads]
            mine = [half_rows(rows, core) for rows in grads]
        else:
            cut = grads.shape[1] // len(weights)
            away, mine = half_rows(grads, 1 - core), half_rows(grads, core)
            away = [away[:, n * cut : (n + 1) * cut] for n in range(len(weights))]
            mine = [mine[:, n * cut : (n + 1) * cut] for n in range(len(weights))]
        away = sum(right_product(rows, weight) for rows, weight in zip(away, weights))
        mine = sum(right_product(rows, weight) for rows, weight in zip(mine, weights))
        away, mine = tick((away.astype(bf16), mine))
        mine = mine + widen(core_swap(away))
        low, mine = tick((mine.astype(bf16), mine))
        arrived = chip_swap(low)
        mine = tick(mine) + widen(arrived)
        return tick(mine).reshape(2, local_rows, width)

    stream_zero = widen(both_halves(tokens))
    cotangent_rows = both_halves(cotangent)
    gathered_mixer = spread(rms_apply(stream_zero, gain_mixer).astype(bf16))
    mixer_x = product(gathered_mixer, mixer_in_x)
    gate_values = product(gathered_mixer, mixer_in_z)

    def conv_part(values, weight, bias_vec):
        return causal_conv(values, weight, bias_vec, documents)

    activated, conv_back = jax.vjp(conv_part, mixer_x, conv_weight, conv_bias)
    act_low = activated.astype(bf16)
    mixer_feats = sum_mp(product(act_low, mixer_proj))
    delta_low = mixer_feats[:, :RANK].astype(bf16)
    delta_pre = product(delta_low, delta_proj) + delta_bias[None, :]
    state_shape = (seq_len, STATE, LANES)
    in_wide = jnp.broadcast_to(mixer_feats[:, RANK : RANK + STATE, None], state_shape)
    out_wide = jnp.broadcast_to(mixer_feats[:, RANK + STATE :, None], state_shape)
    keep_wide = jnp.broadcast_to(carry_on[:, None], (seq_len, LANES))
    decay_rates = -jnp.exp(decay_log.T)
    skip_row = skip_weight[None, :]
    scanned_low, result, states = scan_fwd(
        activated, delta_pre, gate_values, keep_wide, in_wide, out_wide, decay_rates, skip_row
    )
    stream_one = stream_zero + collect(((scanned_low, mixer_out),), product)
    stream_two, kept_first = ffn_forward(stream_one, gain_first, gate_first, up_first, down_first)
    gathered_attn = spread(rms_apply(stream_two, gain_attn).astype(bf16))
    queries = product(gathered_attn, query_weight, bf16)
    key_rows = product(gathered_attn, key_weight, bf16)
    value_rows = product(gathered_attn, value_weight, bf16)
    heads_width = queries.shape[1]
    attended_flat = attend(
        attend_forward_kernel,
        (queries, key_rows, value_rows),
        documents,
        heads_width,
        "attend_forward",
    )
    stream_three = stream_two + collect(((attended_flat, output_weight),), product)
    stream_four, kept_second = ffn_forward(
        stream_three, gain_second, gate_second, up_second, down_second
    )
    mixed_out = lax.dynamic_index_in_dim(stream_four, chip, 0, keepdims=False).astype(bf16)

    own_places = (
        jnp.arange(2, dtype=jnp.int32)[:, None] * (2 * local_rows)
        + core * local_rows
        + jnp.arange(local_rows, dtype=jnp.int32)[None, :]
    )
    live_rows = (own_places < valid_len[0]).astype(f32)
    stream_grad = widen(cotangent_rows) * live_rows[..., None]
    d_branch = spread(stream_grad.astype(bf16))
    push("down_second", packed_grad(kept_second[4], d_branch), down_second.shape[0])
    d_branch = tick(d_branch)
    d_gate, d_up = ffn_pointwise(right_product(d_branch, down_second), kept_second)
    push("gate_second", packed_grad(kept_second[1], d_gate), width)
    push("up_second", packed_grad(kept_second[1], d_up), width)
    d_gate, d_up = tick((d_gate, d_up))
    d_normed = collect_back((d_gate, d_up), (gate_second, up_second))
    stream_grad, d_gain_second = norm_backward(stream_grad, kept_second[0], gain_second, d_normed)
    d_branch = spread(stream_grad.astype(bf16))
    d_attended = right_product(d_branch, output_weight, bf16)
    d_attended = tick(d_attended)
    d_heads = attend(
        attend_backward_kernel,
        (queries, key_rows, value_rows, d_attended),
        documents,
        3 * heads_width,
        "attend_backward",
    )
    heads_rows = width * 3 * heads_width // LANES
    attn_rows = heads_rows + attended_flat.shape[1] * width // LANES
    attn_packed = packed_grad(
        attended_flat,
        d_branch,
        attn_rows,
        heads_rows,
        packed_grad(gathered_attn, d_heads, attn_rows),
    )
    push("attn", attn_packed, 0)
    d_heads = tick(d_heads)
    d_normed = collect_back(d_heads, (query_weight, key_weight, value_weight))
    stream_grad, d_gain_attn = norm_backward(stream_grad, stream_two, gain_attn, d_normed)
    d_branch = spread(stream_grad.astype(bf16))
    d_gate, d_up = ffn_pointwise(right_product(d_branch, down_first), kept_first)
    push("down_first", packed_grad(kept_first[4], d_branch), down_first.shape[0])
    push("gate_first", packed_grad(kept_first[1], d_gate), width)
    push("up_first", packed_grad(kept_first[1], d_up), width)
    d_gate, d_up = tick((d_gate, d_up))
    d_normed = collect_back((d_gate, d_up), (gate_first, up_first))
    stream_grad, d_gain_first = norm_backward(stream_grad, kept_first[0], gain_first, d_normed)
    d_branch = spread(stream_grad.astype(bf16))
    d_scanned = right_product(d_branch, mixer_out)
    channels = mixer_proj.shape[0]
    push("mixer_out", packed_grad(scanned_low, d_branch), channels)
    d_scanned = tick(d_scanned)
    d_scanned = tick(d_scanned)
    scan_inputs = (
        activated, delta_pre, gate_values, result, d_scanned,
        keep_wide, in_wide, out_wide, decay_rates, skip_row, states,
    )
    later = list(scan_bwd(*scan_inputs))
    later[-1] = tick(later[-1])
    (d_act_scan, d_delta_low, d_gate_low, d_in_map, d_out_map, d_rates, grad_skip, d_bias, _) = (
        scan_bwd(*scan_inputs, before=later)
    )
    push("in_z", packed_grad(gathered_mixer, d_gate_low), width)
    d_delta_low = tick(d_delta_low)
    d_feats = sum_mp(
        jnp.concatenate(
            [
                right_product(d_delta_low, delta_proj),
                d_in_map,
                d_out_map,
            ],
            axis=1,
        ).astype(bf16)
    )
    d_feats = tick(d_feats)
    d_activated = d_act_scan + right_product(d_feats, mixer_proj)
    d_mixer_x, grad_conv_weight, grad_conv_bias = conv_back(d_activated)
    d_mixer_x = d_mixer_x.astype(bf16)
    push("in_x", packed_grad(gathered_mixer, d_mixer_x), width, TAIL)
    d_mixer_x = tick(d_mixer_x)
    d_normed = collect_back((d_mixer_x, d_gate_low), (mixer_in_x, mixer_in_z))
    stream_grad, d_gain_mixer = norm_backward(stream_grad, stream_zero, gain_mixer, d_normed)
    input_grad = lax.dynamic_index_in_dim(stream_grad, chip, 0, keepdims=False)
    input_grad = tick(input_grad)
    joint = jnp.concatenate(
        [left_product(act_low, d_feats, bf16), pack(left_product(delta_low, d_delta_low, bf16))]
    )
    joint = widen(sum_dp_small(tick(joint)))
    little = jnp.concatenate(
        [grad_conv_weight, grad_conv_bias[None], d_bias, d_rates * decay_rates, grad_skip]
    )
    little = sum_dp_small(tick(little))
    gain_grads = 0.5 * sum_mp(jnp.stack([d_gain_mixer, d_gain_first, d_gain_attn, d_gain_second]))
    gain_grads = sum_dp_small(tick(gain_grads))
    grad_mixer_proj = joint[:channels]
    grad_delta_proj = unpack(joint[channels:], RANK)

    while queue or any(stream.flying for stream in streams):
        tick()
    unpack_finished(len(wanted))

    return (
        mixed_out,
        input_grad,
        gain_grads[0],
        found["in_x"],
        found["in_z"],
        little[:CONV],
        little[CONV],
        grad_mixer_proj,
        grad_delta_proj,
        little[CONV + 1],
        little[CONV + 2 : CONV + 2 + STATE].T,
        little[CONV + 2 + STATE],
        found["mixer_out"],
        gain_grads[1],
        found["gate_first"],
        found["up_first"],
        found["down_first"],
        gain_grads[2],
        found["query"],
        found["key"],
        found["value"],
        found["output"],
        gain_grads[3],
        found["gate_second"],
        found["up_second"],
        found["down_second"],
    )


def solution(mesh):
    placed = (
        P(("dp", "mp"), None),
        P(("dp", "mp"), None),
        P("dp", None),
        P("dp"),
        P(),
        P(None, "mp"),
        P(None, "mp"),
        P(None, "mp"),
        P("mp"),
        P("mp", None),
        P(None, "mp"),
        P("mp"),
        P("mp", None),
        P("mp"),
        P("mp", None),
        P(),
        P(None, "mp"),
        P(None, "mp"),
        P("mp", None),
        P(),
        P(None, "mp"),
        P(None, "mp"),
        P(None, "mp"),
        P("mp", None),
        P(),
        P(None, "mp"),
        P(None, "mp"),
        P("mp", None),
    )
    return jax.shard_map(
        per_device,
        mesh=mesh,
        in_specs=placed,
        out_specs=(
            P(("dp", "mp"), None),
            P(("dp", "mp"), None),
            P(),
            P(None, "mp"),
            P(None, "mp"),
            P(None, "mp"),
            P("mp"),
            P("mp", None),
            P(None, "mp"),
            P("mp"),
            P("mp", None),
            P("mp"),
            P("mp", None),
            P(),
            P(None, "mp"),
            P(None, "mp"),
            P("mp", None),
            P(),
            P(None, "mp"),
            P(None, "mp"),
            P(None, "mp"),
            P("mp", None),
            P(),
            P(None, "mp"),
            P(None, "mp"),
            P("mp", None),
        ),
        check_vma=False,
    )
```

time: 6230 us -> 996 us (0.16); the launches traced: 6150 us -> 987 us
  other arithmetic: 2400 us -> 45.2 us
  local copies, waits for them, and re-layouts: 1420 us -> 84.9 us
  blocking collectives: 1310 us -> 0 us
  waiting for transfers between devices: 835 us -> 260 us
  Pallas kernels: 0 us -> 263 us
  starting transfers between devices: 3.47 us -> 266 us
  matrix products: 139 us -> 61.5 us
    reduce_sum x610 -> x0, other arithmetic: 1930 us -> none  [the longest x256 931 us: one_block(): factor = jnp.exp(delta_block[position][:, None] * decay_rates)]
    unnamed x1 -> x0, blocking collectives: 1210 us -> none
    all_gather x9 -> x0, waiting for transfers between devices: 625 us -> none  [the longest x1 495 us: reduce_rows(): lax.all_gather(lax.psum_scatter(grid_rows, 'dp', scatter_dimension=0, til...]
    unnamed x280 -> x641, local copies, waits for them, and re-layouts: 473 us -> 65.6 us
    another operation x581 -> x14, local copies, waits for them, and re-layouts: 359 us -> 3.39 us  [the longest x4 1.8 us: per_device(): jnp.stack([d_gain_mixer, d_gain_first, d_gain_attn, d_gain_second])]
    add_any x32 -> x0, other arithmetic: 336 us -> none  [selective_scan(): _, readouts = lax.scan(jax.checkpoint(one_block), initial, pieces)]
    ppermute x0 -> x189, starting transfers between devices: none -> 266 us  [the longest x157 246 us: dp_permute(): return lax.ppermute(v, 'dp', pairs)]
    pallas_call x0 -> x83, Pallas kernels: none -> 263 us  [the longest x54 130 us: round(): pl.pallas_call(body, in_specs=[pl.BlockSpec(memory_space=pltpu.SMEM)] + s...]
where the time goes in v1:
time: 996 us; the launch traced here: 987 us
  starting transfers between devices  266 us (27%)
  Pallas kernels  263 us (26%)
  waiting for transfers between devices  260 us (26%)
  local copies, waits for them, and re-layouts  84.9 us (9%)
  matrix products  61.5 us (6%)
  other arithmetic  45.2 us (5%)
    ppermute x157, starting transfers between devices, dp_permute(): return lax.ppermute(v, 'dp', pairs)  246 us
    ppermute x157, waiting for transfers between devices, dp_permute(): return lax.ppermute(v, 'dp', pairs)  175 us
    pallas_call x54, Pallas kernels, round(): pl.pallas_call(body, in_specs=[pl.BlockSpec(memory_space=pltpu.SMEM)] + s...  130 us
    ppermute x13, waiting for transfers between devices, chip_swap(): return lax.ppermute(v, 'mp', [(0, 2), (2, 0), (1, 3), (3, 1)])  69.5 us
    unnamed x641, local copies, waits for them, and re-layouts  65.6 us
    pallas_call x13, Pallas kernels, unpack_parts(): pl.pallas_call(lambda *refs: unpack_kernel(starts, *refs), grid=(steps,),...  57.3 us
    pallas_call x2, Pallas kernels, scan_bwd(): pl.pallas_call(lambda *refs: scan_bwd_kernel(carried, *refs), grid=(steps...  32.3 us
    dot_general x19, matrix products, product(): return jnp.dot(left_rows, weight, preferred_element_type=f32).astype(kind)  31 us
  transfers between devices with their start and end apart: 189, of which 70 were waited for; matrix products, arithmetic and copies ran while one was open for 9% of the time, Pallas kernels for 24%

profile of v1, /device:TPU:0, one launch (start us, length us, event | category | flops | bytes accessed | tf_op | source)
XLA Modules:
  0.0 987.1 jit_solution(961934085605248136)
XLA Ops:
  3.7 9.4 collective-permute-done
  48.0 14.7 %scan_forward.1 = (bf16[512,768]{1,0:T(8,128)(2,1)S(1)}, f32[512,768]{1,0:T(8,128)S(1)}, f32[512,16,768]{2,1,0:T(8,128)}) custom-call(f32[512,768]{1,0:T(8,128)S(1)} %copy-done.11, f32[512,768]{1,0:T(8,128)S(1)} %convolution_add_fusion.10.pre_ref.refs_1_, f32[512,768]{1,0:T(8,128)S(1)} %copy-done.18, f32[512,128]{1,0:T(8,128)S(1)} %broadcast_in_dim.25.keep_ref.refs_5_, ...), custom_call_target="tpu_custom_call" | custom-call | flops 251658240 | bytes 39321600 | tf_op jit(solution)/shard_map/scan_forward/pallas_call | solution.py:115
  69.1 17.8 %collective-permute-done.5 = bf16[256,1536]{1,0:T(8,128)(2,1)S(1)} collective-permute-done((bf16[256,1536]{1,0:T(8,128)(2,1)S(1)}, bf16[256,1536]{1,0:T(8,128)(2,1)S(1)}, u32[]{:S(2)}, u32[]{:S(2)}) %collective-permute-start.5) | collective-permute-done | bytes 786464 | tf_op jit(solution)/shard_map/ppermute | solution.py:311
  104.8 17.8 %collective-permute-done.8 = bf16[256,1536]{1,0:T(8,128)(2,1)S(1)} collective-permute-done((bf16[256,1536]{1,0:T(8,128)(2,1)S(1)}, bf16[256,1536]{1,0:T(8,128)(2,1)S(1)}, u32[]{:S(2)}, u32[]{:S(2)}) %collective-permute-start.8) | collective-permute-done | bytes 786464 | tf_op jit(solution)/shard_map/ppermute | solution.py:311
  144.6 5.8 collective-permute-done.15
  152.8 13.9 %collective-permute-done.11 = bf16[256,1536]{1,0:T(8,128)(2,1)S(1)} collective-permute-done((bf16[256,1536]{1,0:T(8,128)(2,1)S(1)}, bf16[256,1536]{1,0:T(8,128)(2,1)S(1)}, u32[]{:S(2)}, u32[]{:S(2)}) %collective-permute-start.11) | collective-permute-done | bytes 786464 | tf_op jit(solution)/shard_map/ppermute | solution.py:311
  202.8 5.5 collective-permute-done.18.refs_4_
  224.5 7.9 collective-permute-done.20.refs_5_
  238.2 5.8 collective-permute-done.26.refs_6_
  247.6 7.5 collective-permute-start.39
  286.7 7.8 collective-permute-done.42.refs_7_
  315.4 9.4 collective-permute-done.36.refs_8_
  368.0 6.3 collective-permute-start.79
  448.7 6.8 collective-permute-done.88.refs_9_
  490.0 9.1 unpack.13
  520.4 12.8 %collective-permute-done.96.refs_8_ = bf16[2304,128]{1,0:T(8,128)(2,1)S(1)} collective-permute-done((bf16[2304,128]{1,0:T(8,128)(2,1)S(1)}, bf16[2304,128]{1,0:T(8,128)(2,1)S(1)}, u32[]{:S(2)}, u32[]{:S(2)}) %collective-permute-start.96) | collective-permute-done | bytes 589856 | tf_op jit(solution)/shard_map/ppermute | solution.py:320
  569.1 16.6 %collective-permute-done.100.refs_9_ = bf16[2304,128]{1,0:T(8,128)(2,1)S(1)} collective-permute-done((bf16[2304,128]{1,0:T(8,128)(2,1)S(1)}, bf16[2304,128]{1,0:T(8,128)(2,1)S(1)}, u32[]{:S(2)}, u32[]{:S(2)}) %collective-permute-start.100) | collective-permute-done | bytes 589856 | tf_op jit(solution)/shard_map/ppermute | solution.py:320
  609.5 15.9 %scan_backward.2 = (f32[512,768]{1,0:T(8,128)S(1)}, bf16[512,768]{1,0:T(8,128)(2,1)S(1)}, bf16[512,768]{1,0:T(8,128)(2,1)S(1)}, f32[512,16]{1,0:T(8,128)S(1)}, f...) custom-call(f32[512,768]{1,0:T(8,128)S(1)} %copy-done.12, ...), custom_call_target="tpu_custom_call" | custom-call | flops 629145600 | bytes 39321600 | tf_op jit(solution)/shard_map/scan_backward/pallas_call | solution.py:228
  625.4 16.4 %scan_backward.3 = (f32[512,768]{1,0:T(8,128)S(1)}, bf16[512,768]{1,0:T(8,128)(2,1)S(1)}, bf16[512,768]{1,0:T(8,128)(2,1)S(1)}, f32[512,16]{1,0:T(8,128)S(1)}, f...) custom-call(f32[512,768]{1,0:T(8,128)S(1)} %copy-done.12, ...), custom_call_target="tpu_custom_call", output_to_operand_aliasing={{0}: (12, {}), {1}: (13, {}), {2}: (14, {}), {3}: (15, {}),... | custom-call | flops 629145600 | bytes 39321600 | tf_op jit(solution)/shard_map/scan_backward/pallas_call | solution.py:228
  728.1 5.4 collective-permute-start.154
  809.7 5.8 collective-permute-done.161.refs_9_
  829.2 9.0 collective-permute-done.134.refs_9_
  890.2 10.8 %collective-permute-done.139.refs_6_ = bf16[2304,128]{1,0:T(8,128)(2,1)S(1)} collective-permute-done((bf16[2304,128]{1,0:T(8,128)(2,1)S(1)}, bf16[2304,128]{1,0:T(8,128)(2,1)S(1)}, u32[]{:S(2)}, u32[]{:S(2)}) %collective-permute-start.139) | collective-permute-done | bytes 589856 | tf_op jit(solution)/shard_map/ppermute | solution.py:320
  922.8 9.0 unpack.25
  (1265 shorter events, 732.9 us)
Async XLA Ops:
  220.0 40.3 %collective-permute-start.28 = (bf16[256,1536]{1,0:T(8,128)(2,1)S(1)}, bf16[256,1536]{1,0:T(8,128)(2,1)S(1)}, u32[]{:S(2)}, u32[]{:S(2)}) collective-permute-start(bf16[256,1536]{1,0:T(8,128)(2,1)S(1)} %get-tuple-element.401), channel_id=1, source_target_pairs={{0,2},{2,0},{1,3},{3,1},{4,6},{6,4},{5,7},{7,5},{8,10},{10,8},{9,1... | collective-permute-start | bytes 2359304 | tf_op jit(solution)/shard_map/ppermute | solution.py:311
  264.3 32.5 %collective-permute-start.47 = (bf16[2,128,1536]{2,1,0:T(8,128)(2,1)S(1)}, bf16[2,128,1536]{2,1,0:T(8,128)(2,1)S(1)}, u32[]{:S(2)}, u32[]{:S(2)}) collective-permute-start(bf16[2,128,1536]{2,1,0:T(8,128)(2,1)S(1)} %fusion.38), channel_id=1, source_target_pairs={{0,1},{1,0},{2,3},{3,2},{4,5},{5,4},{6,7},{7,6},{8,9},{9,8},{10,11... | collective-permute-start | bytes 2359304 | tf_op jit(solution)/shard_map/ppermute | solution.py:307
  308.5 31.7 %collective-permute-start.48 = (bf16[256,1536]{1,0:T(8,128)(2,1)S(1)}, bf16[256,1536]{1,0:T(8,128)(2,1)S(1)}, u32[]{:S(2)}, u32[]{:S(2)}) collective-permute-start(bf16[256,1536]{1,0:T(8,128)(2,1)S(1)} %fusion), channel_id=1, source_target_pairs={{0,1},{1,0},{2,3},{3,2},{4,5},{5,4},{6,7},{7,6},{8,9},{9,8},{10,11... | collective-permute-start | bytes 2359304 | tf_op jit(solution)/shard_map/ppermute | solution.py:307
  344.8 36.4 %collective-permute-start.49 = (bf16[256,1536]{1,0:T(8,128)(2,1)S(1)}, bf16[256,1536]{1,0:T(8,128)(2,1)S(1)}, u32[]{:S(2)}, u32[]{:S(2)}) collective-permute-start(bf16[256,1536]{1,0:T(8,128)(2,1)S(1)} %get-tuple-element.433), channel_id=1, source_target_pairs={{0,2},{2,0},{1,3},{3,1},{4,6},{6,4},{5,7},{7,5},{8,10},{10,8},{9,1... | collective-permute-start | bytes 2359304 | tf_op jit(solution)/shard_map/ppermute | solution.py:311
  388.0 34.2 %collective-permute-start.50 = (bf16[2,128,1536]{2,1,0:T(8,128)(2,1)S(1)}, bf16[2,128,1536]{2,1,0:T(8,128)(2,1)S(1)}, u32[]{:S(2)}, u32[]{:S(2)}) collective-permute-start(bf16[2,128,1536]{2,1,0:T(8,128)(2,1)S(1)} %get-tuple-element.753), channel_id=1, source_target_pairs={{0,1},{1,0},{2,3},{3,2},{4,5},{5,4},{6,7},{7,6},{8,9},{9,8},{10,11... | collective-permute-start | bytes 2359304 | tf_op jit(solution)/shard_map/ppermute | solution.py:307
  408.7 30.6 %collective-permute-start.61 = (bf16[2304,128]{1,0:T(8,128)(2,1)S(1)}, bf16[2304,128]{1,0:T(8,128)(2,1)S(1)}, u32[]{:S(2)}, u32[]{:S(2)}) collective-permute-start(bf16[2304,128]{1,0:T(8,128)(2,1)S(1)} %get-tuple-element.445.refs_5_), channel_id=1, source_target_pairs={{0,8},{8,0},{4,12},{12,4},{16,24},{24,16},{20,28},{28,20},{1,9},{9... | collective-permute-start | bytes 1769480 | tf_op jit(solution)/shard_map/ppermute | solution.py:320
  436.7 35.5 %collective-permute-start.84 = (bf16[256,1536]{1,0:T(8,128)(2,1)S(1)}, bf16[256,1536]{1,0:T(8,128)(2,1)S(1)}, u32[]{:S(2)}, u32[]{:S(2)}) collective-permute-start(bf16[256,1536]{1,0:T(8,128)(2,1)S(1)} %fusion.2), channel_id=1, source_target_pairs={{0,1},{1,0},{2,3},{3,2},{4,5},{5,4},{6,7},{7,6},{8,9},{9,8},{10,11... | collective-permute-start | bytes 2359304 | tf_op jit(solution)/shard_map/ppermute | solution.py:307
  475.6 40.5 %collective-permute-start.85 = (bf16[256,1536]{1,0:T(8,128)(2,1)S(1)}, bf16[256,1536]{1,0:T(8,128)(2,1)S(1)}, u32[]{:S(2)}, u32[]{:S(2)}) collective-permute-start(bf16[256,1536]{1,0:T(8,128)(2,1)S(1)} %get-tuple-element.493), channel_id=1, source_target_pairs={{0,2},{2,0},{1,3},{3,1},{4,6},{6,4},{5,7},{7,5},{8,10},{10,8},{9,1... | collective-permute-start | bytes 2359304 | tf_op jit(solution)/shard_map/ppermute | solution.py:311
  505.6 40.5 %collective-permute-start.69 = (bf16[2304,128]{1,0:T(8,128)(2,1)S(1)}, bf16[2304,128]{1,0:T(8,128)(2,1)S(1)}, u32[]{:S(2)}, u32[]{:S(2)}) collective-permute-start(bf16[2304,128]{1,0:T(8,128)(2,1)S(1)} %get-tuple-element.456.refs_4_), channel_id=1, source_target_pairs={{8,16},{16,8},{12,20},{20,12},{9,17},{17,9},{13,21},{21,13},{10,18... | collective-permute-start | bytes 1769480 | tf_op jit(solution)/shard_map/ppermute | solution.py:320
  506.3 40.6 %collective-permute-start.70 = (bf16[2304,128]{1,0:T(8,128)(2,1)}, bf16[2304,128]{1,0:T(8,128)(2,1)}, u32[]{:S(2)}, u32[]{:S(2)}) collective-permute-start(bf16[2304,128]{1,0:T(8,128)(2,1)} %get-tuple-element.457.refs_5_), channel_id=1, source_target_pairs={{0,8},{8,0},{4,12},{12,4},{16,24},{24,16},{20,28},{28,20},{1,9},{9... | collective-permute-start | bytes 1769480 | tf_op jit(solution)/shard_map/ppermute | solution.py:320
  546.9 55.5 %collective-permute-start.101 = (bf16[2,128,1536]{2,1,0:T(8,128)(2,1)}, bf16[2,128,1536]{2,1,0:T(8,128)(2,1)}, u32[]{:S(2)}, u32[]{:S(2)}) collective-permute-start(bf16[2,128,1536]{2,1,0:T(8,128)(2,1)} %get-tuple-element.749), channel_id=1, source_target_pairs={{0,1},{1,0},{2,3},{3,2},{4,5},{5,4},{6,7},{7,6},{8,9},{9,8},{10,11... | collective-permute-start | bytes 2359304 | tf_op jit(solution)/shard_map/ppermute | solution.py:307
  554.6 39.5 %collective-permute-start.72 = (bf16[2304,128]{1,0:T(8,128)(2,1)S(1)}, bf16[2304,128]{1,0:T(8,128)(2,1)S(1)}, u32[]{:S(2)}, u32[]{:S(2)}) collective-permute-start(bf16[2304,128]{1,0:T(8,128)(2,1)S(1)} %get-tuple-element.460.refs_4_), channel_id=1, source_target_pairs={{8,16},{16,8},{12,20},{20,12},{9,17},{17,9},{13,21},{21,13},{10,18... | collective-permute-start | bytes 1769480 | tf_op jit(solution)/shard_map/ppermute | solution.py:320
  555.3 40.3 %collective-permute-start.73 = (bf16[2304,128]{1,0:T(8,128)(2,1)S(1)}, bf16[2304,128]{1,0:T(8,128)(2,1)S(1)}, u32[]{:S(2)}, u32[]{:S(2)}) collective-permute-start(bf16[2304,128]{1,0:T(8,128)(2,1)S(1)} %get-tuple-element.461.refs_5_), channel_id=1, source_target_pairs={{0,8},{8,0},{4,12},{12,4},{16,24},{24,16},{20,28},{28,20},{1,9},{9... | collective-permute-start | bytes 1769480 | tf_op jit(solution)/shard_map/ppermute | solution.py:320
  557.9 38.9 %collective-permute-start.74 = (bf16[2304,128]{1,0:T(8,128)(2,1)S(1)}, bf16[2304,128]{1,0:T(8,128)(2,1)S(1)}, u32[]{:S(2)}, u32[]{:S(2)}) collective-permute-start(bf16[2304,128]{1,0:T(8,128)(2,1)S(1)} %get-tuple-element.462.refs_6_), channel_id=1, source_target_pairs={{0,4},{4,0},{8,12},{12,8},{16,20},{20,16},{24,28},{28,24},{1,5},{5... | collective-permute-start | bytes 1769480 | tf_op jit(solution)/shard_map/ppermute | solution.py:320
  592.6 65.1 %collective-permute-start.106 = (bf16[2304,128]{1,0:T(8,128)(2,1)}, bf16[2304,128]{1,0:T(8,128)(2,1)}, u32[]{:S(2)}, u32[]{:S(2)}) collective-permute-start(bf16[2304,128]{1,0:T(8,128)(2,1)} %get-tuple-element.512.refs_4_), channel_id=1, source_target_pairs={{8,16},{16,8},{12,20},{20,12},{9,17},{17,9},{13,21},{21,13},{10,18... | collective-permute-start | bytes 1769480 | tf_op jit(solution)/shard_map/ppermute | solution.py:320
  594.0 66.7 %collective-permute-start.107 = (bf16[2304,128]{1,0:T(8,128)(2,1)}, bf16[2304,128]{1,0:T(8,128)(2,1)}, u32[]{:S(2)}, u32[]{:S(2)}) collective-permute-start(bf16[2304,128]{1,0:T(8,128)(2,1)} %get-tuple-element.513.refs_5_), channel_id=1, source_target_pairs={{0,8},{8,0},{4,12},{12,4},{16,24},{24,16},{20,28},{28,20},{1,9},{9... | collective-permute-start | bytes 1769480 | tf_op jit(solution)/shard_map/ppermute | solution.py:320
  595.6 65.2 %collective-permute-start.108 = (bf16[2304,128]{1,0:T(8,128)(2,1)}, bf16[2304,128]{1,0:T(8,128)(2,1)}, u32[]{:S(2)}, u32[]{:S(2)}) collective-permute-start(bf16[2304,128]{1,0:T(8,128)(2,1)} %get-tuple-element.514.refs_6_), channel_id=1, source_target_pairs={{0,4},{4,0},{8,12},{12,8},{16,20},{20,16},{24,28},{28,24},{1,5},{5... | collective-permute-start | bytes 1769480 | tf_op jit(solution)/shard_map/ppermute | solution.py:320
  601.0 68.2 %collective-permute-start.112 = (bf16[2304,128]{1,0:T(8,128)(2,1)}, bf16[2304,128]{1,0:T(8,128)(2,1)}, u32[]{:S(2)}, u32[]{:S(2)}) collective-permute-start(bf16[2304,128]{1,0:T(8,128)(2,1)} %get-tuple-element.464.refs_4_), channel_id=1, source_target_pairs={{8,16},{16,8},{12,20},{20,12},{9,17},{17,9},{13,21},{21,13},{10,18... | collective-permute-start | bytes 1769480 | tf_op jit(solution)/shard_map/ppermute | solution.py:320
  697.6 45.2 %collective-permute-start.13 = (bf16[256,1536]{1,0:T(8,128)(2,1)S(1)}, bf16[256,1536]{1,0:T(8,128)(2,1)S(1)}, u32[]{:S(2)}, u32[]{:S(2)}) collective-permute-start(bf16[256,1536]{1,0:T(8,128)(2,1)S(1)} %copy-done.316), channel_id=1, source_target_pairs={{0,1},{1,0},{2,3},{3,2},{4,5},{5,4},{6,7},{7,6},{8,9},{9,8},{10,11... | collective-permute-start | bytes 2359304 | tf_op jit(solution)/shard_map/ppermute | solution.py:307
  735.2 45.2 %collective-permute-start.104 = (bf16[256,1536]{1,0:T(8,128)(2,1)}, bf16[256,1536]{1,0:T(8,128)(2,1)}, u32[]{:S(2)}, u32[]{:S(2)}) collective-permute-start(bf16[256,1536]{1,0:T(8,128)(2,1)} %fusion.3), channel_id=1, source_target_pairs={{0,1},{1,0},{2,3},{3,2},{4,5},{5,4},{6,7},{7,6},{8,9},{9,8},{10,11... | collective-permute-start | bytes 2359304 | tf_op jit(solution)/shard_map/ppermute | solution.py:307
  784.6 40.1 %collective-permute-start.105 = (bf16[256,1536]{1,0:T(8,128)(2,1)}, bf16[256,1536]{1,0:T(8,128)(2,1)}, u32[]{:S(2)}, u32[]{:S(2)}) collective-permute-start(bf16[256,1536]{1,0:T(8,128)(2,1)} %get-tuple-element.557), channel_id=1, source_target_pairs={{0,2},{2,0},{1,3},{3,1},{4,6},{6,4},{5,7},{7,5},{8,10},{10,8},{9,1... | collective-permute-start | bytes 2359304 | tf_op jit(solution)/shard_map/ppermute | solution.py:311
  850.5 33.3 %collective-permute-start.116 = (f32[4,1536]{1,0:T(4,128)S(1)}, f32[4,1536]{1,0:T(4,128)S(1)}, u32[]{:S(2)}, u32[]{:S(2)}) collective-permute-start(f32[4,1536]{1,0:T(4,128)S(1)} %fusion.53), channel_id=1, source_target_pairs={{0,2},{2,0},{1,3},{3,1},{4,6},{6,4},{5,7},{7,5},{8,10},{10,8},{9,1... | collective-permute-start | bytes 73736 | tf_op jit(solution)/shard_map/ppermute | solution.py:311
  884.0 32.0 %collective-permute-start.188 = (bf16[1344,128]{1,0:T(8,128)(2,1)S(1)}, bf16[1344,128]{1,0:T(8,128)(2,1)S(1)}, u32[]{:S(2)}, u32[]{:S(2)}) collective-permute-start(bf16[1344,128]{1,0:T(8,128)(2,1)S(1)} %add.466), channel_id=1, source_target_pairs={{0,16},{16,0},{4,20},{20,4},{8,24},{24,8},{12,28},{28,12},{1,17},{... | collective-permute-start | bytes 1032200 | tf_op jit(solution)/shard_map/ppermute | solution.py:320
  907.8 31.7 %collective-permute-start.118 = (f32[4,1536]{1,0:T(4,128)S(1)}, f32[4,1536]{1,0:T(4,128)S(1)}, u32[]{:S(2)}, u32[]{:S(2)}) collective-permute-start(f32[4,1536]{1,0:T(4,128)S(1)} %add.459), channel_id=1, source_target_pairs={{0,8},{8,0},{4,12},{12,4},{16,24},{24,16},{20,28},{28,20},{1,9},{9... | collective-permute-start | bytes 73736 | tf_op jit(solution)/shard_map/ppermute | solution.py:320
  (485 other events, 4286.7 us)
